TPU v7x, 32 devices: a whole 2x2x4 slice. The times are simulated.
32 devices in a mesh: gx: 8 (over z, y), gy: 4 (over x, core).
Axes of the slice: x: 2, y: 2, z: 4, core: 2. Of those that a mesh axis runs over, the one named last changes fastest.
Arguments:
- density: float32 [256, 128, 512], P('gx', 'gy'), may hold values from 0.5 to 2
- momentum: float32 [3, 256, 128, 512], P(None, 'gx', 'gy'), may hold values from -3 to 3
- energy: float32 [256, 128, 512], P('gx', 'gy'), may hold values from 2 to 4
- coarse_rows: float32 [2, 2048, 4, 160], P(None, 'gx', 'gy'), may hold values from -2 to 4, as said below
- ghost_rows: int32 [4, 8, 128], P('gy'), may hold values from 0 to 2047, as said below
- time_index: int32 [4, 8, 128], P('gy'), may hold values from 0 to 8
Outputs:
- section_state: float32 [5, 256, 128, 512], P(None, 'gx', 'gy')
Inputs may be any that keep to these rules, and one draw needn't show every extreme that they name: `ghost_rows`: entry [b, a, s] names a coarse row of column b; rows c * 256 to (c + 1) * 256 - 1 of a column lie on the device with gx index c. Exactly 16 of one device's slots name rows held by each source device. `coarse_rows`: field 0 of every row (density) lies in 0.5 to 2.
All inputs are finite; a program needn't handle non-finite values.
Results may differ from a plain program's by a relative error of at most 0.0003.
Values sent between devices are 32-bit elements; how exact they have to be, the bound alone decides.
A program may use at most 256 MiB of HBM per device.

v0:
```python
import math

import jax
import jax.numpy as jnp
from jax import lax
from jax.sharding import PartitionSpec as P

beta_coef = 1.0 / 3.0
a_coef = 14.0 / 9.0
b_coef = 1.0 / 9.0
gamma_gas = 1.4
time_step = 0.4
root_scale = math.sqrt(1.0 - 4.0 * beta_coef * beta_coef)
root_value = (-1.0 + root_scale) / (2.0 * beta_coef)
root_log = math.log(-root_value)
highest = lax.Precision.HIGHEST


def with_halo(block, sides, width):
    for axis, dim in sides:
        count = lax.axis_size(axis)
        forward = [(i, i + 1) for i in range(count - 1)]
        backward = [(target, source) for source, target in forward]
        low = lax.ppermute(
            lax.slice_in_dim(block, block.shape[dim] - width, None, axis=dim), axis, forward
        )
        high = lax.ppermute(lax.slice_in_dim(block, 0, width, axis=dim), axis, backward)
        block = jnp.concatenate([low, block, high], axis=dim)
    return block


def from_behind(array, axis, by):
    peers = lax.axis_size(axis)
    pairs = [(i, i + by) for i in range(peers) if 0 <= i + by < peers]
    return lax.ppermute(array, axis, pairs)


def fluxes(fields, direction):
    density = fields[0]
    carried = fields[1 + direction]
    velocity = carried / density
    kinetic = (fields[1] * fields[1] + fields[2] * fields[2] + fields[3] * fields[3]) / density
    pressure = (gamma_gas - 1.0) * (fields[4] - 0.5 * kinetic)
    columns = [carried]
    for component in range(3):
        product_term = fields[1 + component] * velocity
        if component == direction:
            product_term = product_term + pressure
        columns.append(product_term)
    columns.append((fields[4] + pressure) * velocity)
    return jnp.stack(columns)


def stencil(extended, line_axis, length):

    def window(offset):
        return lax.slice_in_dim(extended, offset, offset + length, axis=line_axis)

    return 0.5 * a_coef * (window(3) - window(1)) + 0.25 * b_coef * (window(4) - window(0))


def root_power(exponent):
    exponent = jnp.asarray(exponent, jnp.int32)
    signs = (1 - 2 * (exponent % 2)).astype(jnp.float32)
    return signs * jnp.exp(exponent.astype(jnp.float32) * root_log)


def inverse_entry(row_index, col_index, length):
    inside = (row_index >= 0) & (row_index < length) & (col_index >= 0) & (col_index < length)
    row_safe = jnp.clip(row_index, 0, length - 1)
    col_safe = jnp.clip(col_index, 0, length - 1)
    smaller = jnp.minimum(row_safe, col_safe)
    larger = jnp.maximum(row_safe, col_safe)
    entry_value = (
        root_power(larger - smaller)
        * (1.0 - root_power(2 * smaller + 2))
        * (1.0 - root_power(2 * (length - larger)))
    )
    entry_value = entry_value / (root_scale * (1.0 - root_power(2 * length + 2)))
    return jnp.where(inside, entry_value, 0.0)


def local_inverse(length):
    positions = jnp.arange(length, dtype=jnp.int32)
    return inverse_entry(positions[:, None], positions[None, :], length)


def edge_flux(extended, direction, line_axis, place, cells_side, length):
    positions = place * cells_side - 2 + jnp.arange(cells_side + 4, dtype=jnp.int32)
    valid = (positions >= 0) & (positions < length)
    shape = [1, 1, 1, 1]
    shape[line_axis] = cells_side + 4
    valid = valid.reshape(shape)
    safe = jnp.where(valid, extended, 1.0)
    return jnp.where(valid, fluxes(safe, direction), 0.0)


def add_interfaces(running, portion, first_block, device, cells_side, length):
    blocks = first_block + jnp.arange(portion.shape[0], dtype=jnp.int32)
    last_prev = device * cells_side - 1
    first_next = (device + 1) * cells_side
    before_rows = blocks * cells_side - 1
    after_rows = (blocks + 1) * cells_side
    coef_head_prev = -beta_coef * inverse_entry(last_prev, before_rows, length)
    coef_tail_prev = -beta_coef * inverse_entry(last_prev, after_rows, length) + (
        blocks == device - 1
    ).astype(jnp.float32)
    coef_head_next = -beta_coef * inverse_entry(first_next, before_rows, length) + (
        blocks == device + 1
    ).astype(jnp.float32)
    coef_tail_next = -beta_coef * inverse_entry(first_next, after_rows, length)
    head_values = portion[:, 0]
    tail_values = portion[:, 1]
    previous = (
        running[0]
        + jnp.einsum("j,jfoz->foz", coef_head_prev, head_values, precision=highest)
        + jnp.einsum("j,jfoz->foz", coef_tail_prev, tail_values, precision=highest)
    )
    following = (
        running[1]
        + jnp.einsum("j,jfoz->foz", coef_head_next, head_values, precision=highest)
        + jnp.einsum("j,jfoz->foz", coef_tail_next, tail_values, precision=highest)
    )
    return (previous, following)


def local(density, momentum, energy, coarse_rows, ghost_rows, time_index):
    fields = jnp.concatenate([density[None], momentum, energy[None]], axis=0)
    cells_side = density.shape[0]
    cells_z = density.shape[2]
    groups_x = lax.axis_size("gx")
    groups_y = lax.axis_size("gy")
    place_x = lax.axis_index("gx")
    place_y = lax.axis_index("gy")
    capacity = 4 * cells_side // groups_x
    coarse_block = coarse_rows.shape[1]
    slot_rows = ghost_rows[0]
    weights_all = time_index[0].astype(jnp.float32) * 0.125
    slot_used = slot_rows >= 0
    owners = jnp.where(slot_used, slot_rows // coarse_block, -1)
    from_self = (slot_used & (owners == place_x)).astype(jnp.int32)
    slot_rank = jnp.cumsum(from_self, axis=1) - 1
    positions = jnp.arange(capacity, dtype=jnp.int32)
    selector = from_self[:, None, :] * (slot_rank[:, None, :] == positions[None, :, None]).astype(
        jnp.int32
    )
    local_rows = jnp.sum(selector * (slot_rows - place_x * coarse_block)[:, None, :], axis=2)
    filled = jnp.sum(selector, axis=2) > 0
    flat_rows = jnp.where(filled, local_rows, 0).reshape(-1)
    level_old = jnp.where(
        filled[:, :, None], coarse_rows[0, :, 0, :][flat_rows].reshape(groups_x, capacity, -1), 0.0
    )
    level_new = jnp.where(
        filled[:, :, None], coarse_rows[1, :, 0, :][flat_rows].reshape(groups_x, capacity, -1), 0.0
    )
    own_rows = lax.dynamic_index_in_dim(slot_rows, place_x, 0, keepdims=False)
    own_weight = lax.dynamic_index_in_dim(weights_all, place_x, 0, keepdims=False)[:, None]
    own_used = own_rows >= 0
    own_owner = jnp.where(own_used, own_rows // coarse_block, -1)
    sources = jnp.arange(groups_x, dtype=jnp.int32)
    matches = (own_owner[None, :] == sources[:, None]).astype(jnp.int32)
    arrival_rank = jnp.sum(matches * jnp.cumsum(matches, axis=1), axis=0) - 1
    slot_index = jnp.where(own_used, own_owner * capacity + arrival_rank, 0)
    paired = jnp.stack([level_old, level_new], axis=1)
    received = lax.all_to_all(paired, "gx", split_axis=0, concat_axis=0, tiled=True)
    arrived_old = received[:, 0].reshape(groups_x * capacity, -1)[slot_index]
    arrived_new = received[:, 1].reshape(groups_x * capacity, -1)[slot_index]
    ghosts = (1.0 - own_weight) * arrived_old + own_weight * arrived_new
    ghosts = jnp.where(own_used[:, None], ghosts, 0.0).reshape(2, 2, cells_side, 5, cells_side)
    below_z = ghosts[0].transpose(2, 1, 3, 0)
    above_z = ghosts[1].transpose(2, 1, 3, 0)
    length_x = cells_side * groups_x
    length_y = cells_side * groups_y
    rimmed = with_halo(fields, (("gx", 1), ("gy", 2)), 2)
    extended_x = jnp.concatenate([rimmed[:, 0:2, 2:-2], fields, rimmed[:, -2:, 2:-2]], axis=1)
    extended_y = jnp.concatenate([rimmed[:, 2:-2, 0:2], fields, rimmed[:, 2:-2, -2:]], axis=2)
    extended_z = jnp.concatenate([below_z, fields, above_z], axis=3)
    block_inverse = local_inverse(cells_side)
    right_x = stencil(edge_flux(extended_x, 0, 1, place_x, cells_side, length_x), 1, cells_side)
    right_y = stencil(edge_flux(extended_y, 1, 2, place_y, cells_side, length_y), 2, cells_side)
    local_x = jnp.einsum("ij,fjyz->fiyz", block_inverse, right_x, precision=highest)
    local_y = jnp.einsum("ij,fxjz->fxiz", block_inverse, right_y, precision=highest)
    bounds_x = jnp.stack([local_x[:, 0], local_x[:, -1]], axis=0)[None]
    bounds_y = jnp.stack([local_y[:, :, 0], local_y[:, :, -1]], axis=0)[None]
    zeros_x = (
        jnp.zeros(bounds_x.shape[2:], jnp.float32),
        jnp.zeros(bounds_x.shape[2:], jnp.float32),
    )
    zeros_y = (
        jnp.zeros(bounds_y.shape[2:], jnp.float32),
        jnp.zeros(bounds_y.shape[2:], jnp.float32),
    )

    def fold_x(running, portion, first_block):
        return add_interfaces(running, portion, first_block, place_x, cells_side, length_x)

    def fold_y(running, portion, first_block):
        return add_interfaces(running, portion, first_block, place_y, cells_side, length_y)

    below_x = from_behind(bounds_x, "gx", 1)
    above_x = from_behind(bounds_x, "gx", -1)
    below_y = from_behind(bounds_y, "gy", 1)
    above_y = from_behind(bounds_y, "gy", -1)
    pair_x = fold_x(
        fold_x(fold_x(zeros_x, below_x, place_x - 1), bounds_x, place_x), above_x, place_x + 1
    )
    pair_y = fold_y(
        fold_y(fold_y(zeros_y, below_y, place_y - 1), bounds_y, place_y), above_y, place_y + 1
    )
    coupling_first = beta_coef * block_inverse[:, 0]
    coupling_last = beta_coef * block_inverse[:, -1]
    deriv_x = (
        local_x
        - coupling_first[None, :, None, None] * pair_x[0][:, None]
        - coupling_last[None, :, None, None] * pair_x[1][:, None]
    )
    deriv_y = (
        local_y
        - coupling_first[None, None, :, None] * pair_y[0][:, :, None]
        - coupling_last[None, None, :, None] * pair_y[1][:, :, None]
    )
    right_z = stencil(fluxes(extended_z, 2), 3, cells_z)
    deriv_z = jnp.dot(
        right_z.reshape(-1, cells_z), local_inverse(cells_z), precision=highest
    ).reshape(right_z.shape)
    return fields - time_step * (deriv_x + deriv_y + deriv_z)


def solution(mesh):
    return jax.shard_map(
        local,
        mesh=mesh,
        in_specs=(
            P("gx", "gy", None),
            P(None, "gx", "gy", None),
            P("gx", "gy", None),
            P(None, "gx", "gy", None),
            P("gy", None, None),
            P("gy", None, None),
        ),
        out_specs=P(None, "gx", "gy", None),
        check_vma=False,
    )
```

profile of v0, /device:TPU:0, one launch (start us, length us, event | category | flops | bytes accessed | tf_op | source)
XLA Modules:
  0.0 312.9 jit_solution(12801647899628170636)
XLA Ops:
  0.0 10.6 %pad_maximum_fusion.2 = f32[5,32,32,512]{3,2,0,1:T(8,128)} fusion(f32[1,32,32,512]{3,2,0,1:T(8,128)} %bitcast.232, f32[1,32,32,512]{3,2,0,1:T(8,128)} %bitcast.237, f32[3,32,32,512]{3,2,1,0:T(8,128)} %param.7), kind=kLoop, calls=%fused_computation.28 | loop fusion | flops 5242880 | bytes 20971520 | tf_op jit(solution)/shard_map/concatenate | solution.py:128
  10.6 2.4 fusion.175
  13.0 1.3 collective-permute-start.1
  14.3 6.4 %collective-permute-start = (f32[5,2,32,512]{3,2,0,1:T(8,128)S(1)}, f32[5,2,32,512]{3,2,0,1:T(8,128)}, u32[]{:S(2)}, u32[]{:S(2)}) collective-permute-start(f32[5,2,32,512]{3,2,0,1:T(8,128)S(1)} %get-tuple-element.30), channel_id=1, source_target_pairs={{0,4},{4,8},{8,12},{12,16},{16,20},{20,24},{24,28},{1,5},{5,9},{9,... | collective-permute-start | bytes 1966088 | tf_op jit(solution)/shard_map/ppermute | solution.py:24
  20.7 1.0 fusion.176
  25.1 5.5 %all-to-all-start = ((f32[8,2,16,160]{3,2,1,0:T(8,128)}), f32[8,2,16,160]{3,2,1,0:T(8,128)S(1)}, u32[]{:S(2)}, u32[]{:S(2)}) async-start(f32[8,2,16,160]{3,2,1,0:T(8,128)} %pad_maximum_fusion.3), calls=%async_computation | async-start | bytes 524288 | tf_op jit(solution)/shard_map/all_to_all | solution.py:165
  35.8 14.1 %all-to-all-done = f32[8,2,16,160]{3,2,1,0:T(8,128)S(1)} async-done(((f32[8,2,16,160]{3,2,1,0:T(8,128)}), f32[8,2,16,160]{3,2,1,0:T(8,128)S(1)}, u32[]{:S(2)}, u32[]{:S(2)}) %all-to-all-start) | async-done | bytes 163872 | tf_op jit(solution)/shard_map/all_to_all | solution.py:165
  51.7 2.5 copy.152
  54.3 2.5 copy.150
  56.8 9.5 %pad_maximum_fusion = f32[5,32,32,516]{3,2,0,1:T(8,128)S(1)} fusion(f32[5,32,32,2]{3,2,0,1:T(8,128)} %bitcast.245, f32[1,32,32,512]{3,2,0,1:T(8,128)S(1)} %bitcast.234, f32[1,32,32,512]{3,2,0,1:T(8,128)} %bitcast.238, f32[5,32,32,2]{3,2,0,1:T(8,128)} %bitcast.246, f32[3,32,32,512]{3,2,1,0:T(8,128)} %param.7), kind=kLoop, calls=%fused_computation.5 | loop fusion | flops 10567680 | bytes 21135360 | tf_op jit(solution)/shard_map/concatenate | solution.py:177
  67.2 5.1 %copy-done.6 = f32[5,32,32,516]{3,2,0,1:T(8,128)} copy-done((f32[5,32,32,516]{3,2,0,1:T(8,128)}, f32[5,32,32,516]{3,2,0,1:T(8,128)S(1)}, u32[]{:S(2)}) %copy-start.6) | copy-done | bytes 10567704
  72.4 2.0 multiply_dynamic-update-slice_fusion.1
  74.3 2.7 copy-done
  77.0 3.1 %add_dynamic-update-slice_fusion = (f32[5,32,32,516]{3,2,0,1:T(8,128)}, f32[1,32,32,516]{3,2,0,1:T(8,128)}) fusion(f32[5,32,32,516]{3,2,0,1:T(8,128)} %multiply_dynamic-update-slice_fusion.1, f32[1,32,32,516]{3,2,0,1:T(8,128)S(1)} %get-tuple-element.10, f32[5,32,32,516]{3,2,0,1:T(8,128)S(1)} %pad_maximum_fusion), kind=kLoop, calls=%fused_computation.42 | loop fusion | flops 5812224 | bytes 17924096
  80.2 8.9 %broadcast_select_fusion.2 = (f32[5,36,32,512]{3,2,0,1:T(8,128)S(1)}, f32[5,36,32,512]{3,2,0,1:T(8,128)}) fusion(pred[36]{0:T(512)(128)(4,1)S(1)} %compare_and_fusion.1, f32[5,2,32,512]{3,2,0,1:T(8,128)} %collective-permute-done.1, f32[1,32,32,512]{3,2,0,1:T(8,128)} %bitcast.233, f32[1,32,32,512]{3,2,0,1:T(8,128)} %bitcast.239, ...), kind=kLoop, calls=%fused_computation.35 | loop fusion | flops 14745600 | bytes 35389476 | tf_op jit(solution)/shard_map/jit(_where)/select_n | solution.py:94
  89.1 3.5 %fusion.173 = (f32[5,36,2,512]{3,2,0,1:T(2,128)S(1)}, f32[5,36,2,512]{3,2,0,1:T(2,128)S(1)}) fusion(f32[5,36,32,512]{3,2,0,1:T(8,128)} %get-tuple-element.23), kind=kLoop, calls=%fused_computation.280 | loop fusion | bytes 2949120 | tf_op jit(solution)/shard_map/slice | solution.py:25
  92.5 1.1 copy.134
  93.7 2.8 collective-permute-start.4
  96.5 1.1 copy.136
  97.6 1.5 collective-permute-start.5
  99.1 1.7 slice_dynamic-update-slice_fusion.2
  100.8 2.6 add_dynamic-update-slice_fusion.2
  103.4 2.1 multiply_dynamic-update-slice_fusion.8
  105.6 2.0 multiply_dynamic-update-slice_fusion.7
  107.6 2.3 multiply_dynamic-update-slice_fusion.6
  109.9 11.5 %broadcast_select_fusion.1 = f32[5,36,32,512]{3,2,0,1:T(8,128)} fusion(f32[5,36,32,512]{3,2,0,1:T(8,128)} %multiply_dynamic-update-slice_fusion.6, pred[36]{0:T(512)(128)(4,1)S(1)} %compare_and_fusion.1), kind=kLoop, calls=%fused_computation.34 | loop fusion | flops 2949120 | bytes 23592996 | tf_op jit(solution)/shard_map/jit(_where)/select_n | solution.py:95
  121.4 15.6 %fusion.17 = f32[5,32,32,512]{3,2,0,1:T(8,128)S(1)} fusion(f32[5,36,32,512]{3,2,0,1:T(8,128)} %broadcast_select_fusion.1), kind=kLoop, calls=%fused_computation.25 | loop fusion | flops 13107200 | bytes 52428800 | tf_op jit(solution)/shard_map/add | solution.py:59
  137.0 17.2 %fusion.19 = f32[5,32,512,32]{2,3,1,0:T(8,128)} fusion(f32[5,32,32,512]{3,2,0,1:T(8,128)S(1)} %fusion.17, s32[32]{0:T(128)S(1)} %iota_clamp_fusion.1, pred[32]{0:T(512)(128)(4,1)S(1)} %iota_compare_fusion.3), kind=kOutput, calls=%fused_computation.30 | convolution fusion | flops 1006699520 | bytes 20971680 | tf_op jit(solution)/shard_map/ij,fjyz->fiyz/dot_general | solution.py:181
  154.2 14.3 %copy.194 = f32[5,32,512,32]{2,1,0,3:T(8,128)} copy(f32[5,32,512,32]{2,3,1,0:T(8,128)} %fusion.19) | data formatting | bytes 20971520 | tf_op jit(solution)/shard_map/ij,fjyz->fiyz/dot_general | solution.py:181
  168.5 1.1 slice_bitcast_fusion.1
  169.7 1.3 collective-permute-start.3
  171.0 5.8 %collective-permute-start.2 = (f32[1,2,5,32,512]{4,3,2,1,0:T(8,128)S(1)}, f32[1,2,5,32,512]{4,3,2,1,0:T(8,128)}, u32[]{:S(2)}, u32[]{:S(2)}) collective-permute-start(f32[1,2,5,32,512]{4,3,2,1,0:T(8,128)S(1)} %maximum_bitcast_fusion), channel_id=1, source_target_pairs={{0,4},{4,8},{8,12},{12,16},{16,20},{20,24},{24,28},{1,5},{5,9},{9,... | collective-permute-start | bytes 1966088 | tf_op jit(solution)/shard_map/ppermute | solution.py:35
  176.8 4.4 %maximum_select_fusion = f32[5,32,36,512]{3,2,0,1:T(8,128)S(1)} fusion(f32[1,32,32,512]{3,2,0,1:T(8,128)S(1)} %bitcast.235, f32[1,32,32,512]{3,2,0,1:T(8,128)S(1)} %bitcast.241, pred[36]{0:T(512)(128)(4,1)S(1)} %compare_and_fusion, f32[5,36,2,512]{3,2,1,0:T(2,128)} %collective-permute-done.4, f32[5,36,2,512]{3,2,1,0:T(2,128)} %collective-permute-done.5, ...), kind=kLoop, calls=%fused_computation.4 | loop fusion | flops 14745600 | bytes 23592996 | tf_op jit(solution)/shard_map/jit(_where)/select_n | solution.py:94
  181.2 1.7 slice_dynamic-update-slice_fusion.1
  182.9 2.5 multiply_dynamic-update-slice_fusion.5
  185.4 3.1 add_dynamic-update-slice_fusion.1
  188.5 2.2 multiply_dynamic-update-slice_fusion.4
  190.7 2.5 multiply_dynamic-update-slice_fusion.3
  193.1 11.3 %broadcast_select_fusion = f32[5,32,36,512]{3,2,0,1:T(8,128)} fusion(f32[5,32,36,512]{3,2,0,1:T(8,128)} %multiply_dynamic-update-slice_fusion.3, pred[36]{0:T(512)(128)(4,1)S(1)} %compare_and_fusion), kind=kLoop, calls=%fused_computation.33 | loop fusion | flops 2949120 | bytes 23592996 | tf_op jit(solution)/shard_map/jit(_where)/select_n | solution.py:95
  204.4 29.5 %fusion.25 = f32[5,32,32,512]{3,2,0,1:T(8,128)} fusion(f32[5,32,36,512]{3,2,0,1:T(8,128)} %broadcast_select_fusion, s32[32]{0:T(128)S(1)} %iota_clamp_fusion.1, pred[32]{0:T(512)(128)(4,1)S(1)} %iota_compare_fusion.3), kind=kOutput, calls=%fused_computation.40 | convolution fusion | flops 1019806720 | bytes 52430848 | tf_op jit(solution)/shard_map/ij,fxjz->fxiz/dot_general | solution.py:182
  233.9 3.2 %fusion.174 = (f32[5,32,1,512]{3,2,0,1:T(1,128)S(1)}, f32[5,32,1,512]{3,2,0,1:T(1,128)S(1)}) fusion(f32[5,32,32,512]{3,2,0,1:T(8,128)} %fusion.25), kind=kLoop, calls=%fused_computation.281 | loop fusion | bytes 1310720 | tf_op jit(solution)/shard_map/slice | solution.py:184
  237.2 1.3 collective-permute-start.7
  238.5 3.6 %collective-permute-start.6 = (f32[1,2,5,32,512]{4,3,2,1,0:T(8,128)S(1)}, f32[1,2,5,32,512]{4,3,2,1,0:T(8,128)S(1)}, u32[]{:S(2)}, u32[]{:S(2)}) collective-permute-start(f32[1,2,5,32,512]{4,3,2,1,0:T(8,128)S(1)} %maximum_bitcast_fusion.1), channel_id=1, source_target_pairs={{0,1},{1,2},{2,3},{4,5},{5,6},{6,7},{8,9},{9,10},{10,11},{12,13},{... | collective-permute-start | bytes 1966088 | tf_op jit(solution)/shard_map/ppermute | solution.py:35
  242.2 3.9 %multiply_dynamic-update-slice_fusion = f32[5,32,32,516]{3,2,0,1:T(8,128)} fusion(f32[5,32,32,516]{3,2,0,1:T(8,128)} %get-tuple-element.7, f32[1,32,32,516]{3,2,0,1:T(8,128)S(1)} %get-tuple-element.10, f32[1,32,32,516]{3,2,0,1:T(8,128)S(1)} %copy-done.5, f32[5,32,32,516]{3,2,0,1:T(8,128)} %copy-done), kind=kLoop, calls=%fused_computation.41 | loop fusion | flops 1056768 | bytes 9469952 | tf_op jit(solution)/shard_map/stack | solution.py:51
  246.1 2.4 add_bitcast_fusion.2
  248.5 2.2 add_bitcast_fusion.3
  251.6 50.6 %multiply_subtract_fusion = f32[5,32,32,512]{3,2,0,1:T(8,128)} fusion(f32[5,32,32,512]{3,2,0,1:T(8,128)} %fusion.25, f32[5,32,512]{2,0,1:T(8,128)S(1)} %copy.144, f32[32]{0:T(128)S(1)} %get-tuple-element.39, f32[5,32,512]{2,0,1:T(8,128)S(1)} %copy.143, f32[32]{0:T(128)S(1)} %get-tuple-element.38, f32[5,32,512]{2,1,0:T(8,128)} %add_bitcast_fusion.2, ...), kind=kOutput, calls=%fused_computation.32 | convolution fusion | flops 16172974080 | bytes 85597184 | tf_op jit(solution)/shard_map/dot_general | solution.py:223
  302.2 10.5 %copy.155 = f32[5,32,32,512]{3,2,1,0:T(8,128)} copy(f32[5,32,32,512]{3,2,0,1:T(8,128)} %multiply_subtract_fusion) | data formatting | bytes 20971520 | tf_op jit(solution)/shard_map/sub | solution.py:226
  (76 shorter events, 7.6 us)
Async XLA Ops:
  0.0 21.8 %copy-start.7 = (s32[1,8,128]{2,1,0:T(8,128)S(1)}, s32[1,8,128]{2,1,0:T(8,128)}, u32[]{:S(2)}) copy-start(s32[1,8,128]{2,1,0:T(8,128)} %param.10) | copy-start | bytes 12292
  10.6 25.0 %copy-start.8 = (s32[1,8,128]{2,1,0:T(8,128)S(1)}, s32[1,8,128]{2,1,0:T(8,128)}, u32[]{:S(2)}) copy-start(s32[1,8,128]{2,1,0:T(8,128)} %param.11) | copy-start | bytes 12292
  10.6 46.2 %copy-start.1 = (f32[32,32,512]{2,1,0:T(8,128)S(1)}, f32[32,32,512]{2,1,0:T(8,128)}, u32[]{:S(2)}) copy-start(f32[32,32,512]{2,1,0:T(8,128)} %param.8) | copy-start | bytes 6291460
  13.0 67.2 %collective-permute-start.1 = (f32[5,2,32,512]{3,2,0,1:T(8,128)}, f32[5,2,32,512]{3,2,0,1:T(8,128)}, u32[]{:S(2)}, u32[]{:S(2)}) collective-permute-start(f32[5,2,32,512]{3,2,0,1:T(8,128)} %get-tuple-element.31), channel_id=1, source_target_pairs={{4,0},{8,4},{12,8},{16,12},{20,16},{24,20},{28,24},{5,1},{9,5},{13... | collective-permute-start | bytes 1966088 | tf_op jit(solution)/shard_map/ppermute | solution.py:27
  14.3 65.9 %collective-permute-start = (f32[5,2,32,512]{3,2,0,1:T(8,128)S(1)}, f32[5,2,32,512]{3,2,0,1:T(8,128)}, u32[]{:S(2)}, u32[]{:S(2)}) collective-permute-start(f32[5,2,32,512]{3,2,0,1:T(8,128)S(1)} %get-tuple-element.30), channel_id=1, source_target_pairs={{0,4},{4,8},{8,12},{12,16},{16,20},{20,24},{24,28},{1,5},{5,9},{9,... | collective-permute-start | bytes 1966088 | tf_op jit(solution)/shard_map/ppermute | solution.py:24
  25.1 24.8 %all-to-all-start = ((f32[8,2,16,160]{3,2,1,0:T(8,128)}), f32[8,2,16,160]{3,2,1,0:T(8,128)S(1)}, u32[]{:S(2)}, u32[]{:S(2)}) async-start(f32[8,2,16,160]{3,2,1,0:T(8,128)} %pad_maximum_fusion.3), calls=%async_computation | async-start | bytes 524288 | tf_op jit(solution)/shard_map/all_to_all | solution.py:165
  66.3 10.7 %copy-start = (f32[5,32,32,516]{3,2,0,1:T(8,128)}, f32[5,32,32,516]{3,2,0,1:T(8,128)S(1)}, u32[]{:S(2)}) copy-start(f32[5,32,32,516]{3,2,0,1:T(8,128)S(1)} %pad_maximum_fusion) | copy-start | bytes 31703044
  67.2 5.1 %copy-start.6 = (f32[5,32,32,516]{3,2,0,1:T(8,128)}, f32[5,32,32,516]{3,2,0,1:T(8,128)S(1)}, u32[]{:S(2)}) copy-start(f32[5,32,32,516]{3,2,0,1:T(8,128)S(1)} %get-tuple-element.9) | copy-start | bytes 31703044
  72.4 7.8 %slice-start = ((s8[6291456]{0:T(1024)(128)(4,1)}), s8[4194304]{0:T(1024)(128)(4,1)S(1)}, s32[]{:S(2)}) async-start(s8[6291456]{0:T(1024)(128)(4,1)} %bitcast.230), calls=%async_computation.1 | async-start | bytes 8388608
  77.0 3.2 %slice-start.1 = ((s8[6291456]{0:T(1024)(128)(4,1)}), s8[2097152]{0:T(1024)(128)(4,1)S(1)}, s32[]{:S(2)}) async-start(s8[6291456]{0:T(1024)(128)(4,1)} %bitcast.230), calls=%async_computation.2 | async-start | bytes 4194304
  93.7 83.1 %collective-permute-start.4 = (f32[5,36,2,512]{3,2,1,0:T(2,128)}, f32[5,36,2,512]{3,2,1,0:T(2,128)}, u32[]{:S(2)}, u32[]{:S(2)}) collective-permute-start(f32[5,36,2,512]{3,2,1,0:T(2,128)} %copy.134), channel_id=1, source_target_pairs={{0,1},{1,2},{2,3},{4,5},{5,6},{6,7},{8,9},{9,10},{10,11},{12,13},{... | collective-permute-start | bytes 2211848 | tf_op jit(solution)/shard_map/ppermute | solution.py:24
  97.6 79.2 %collective-permute-start.5 = (f32[5,36,2,512]{3,2,1,0:T(2,128)}, f32[5,36,2,512]{3,2,1,0:T(2,128)}, u32[]{:S(2)}, u32[]{:S(2)}) collective-permute-start(f32[5,36,2,512]{3,2,1,0:T(2,128)} %copy.136), channel_id=1, source_target_pairs={{1,0},{2,1},{3,2},{5,4},{6,5},{7,6},{9,8},{10,9},{11,10},{13,12},{... | collective-permute-start | bytes 2211848 | tf_op jit(solution)/shard_map/ppermute | solution.py:27
  154.2 22.6 %copy-start.2 = (f32[32,32,512]{2,1,0:T(8,128)S(1)}, f32[32,32,512]{2,1,0:T(8,128)}, u32[]{:S(2)}) copy-start(f32[32,32,512]{2,1,0:T(8,128)} %param.8) | copy-start | bytes 6291460
  154.2 22.6 %copy-start.4 = (f32[32,32,512]{2,1,0:T(8,128)S(1)}, f32[32,32,512]{2,1,0:T(8,128)}, u32[]{:S(2)}) copy-start(f32[32,32,512]{2,1,0:T(8,128)} %param.6) | copy-start | bytes 6291460
  169.7 76.4 %collective-permute-start.3 = (f32[1,2,5,32,512]{4,3,2,1,0:T(8,128)S(1)}, f32[1,2,5,32,512]{4,3,2,1,0:T(8,128)}, u32[]{:S(2)}, u32[]{:S(2)}) collective-permute-start(f32[1,2,5,32,512]{4,3,2,1,0:T(8,128)S(1)} %maximum_bitcast_fusion), channel_id=1, source_target_pairs={{4,0},{8,4},{12,8},{16,12},{20,16},{24,20},{28,24},{5,1},{9,5},{13... | collective-permute-start | bytes 1966088 | tf_op jit(solution)/shard_map/ppermute | solution.py:35
  171.0 75.1 %collective-permute-start.2 = (f32[1,2,5,32,512]{4,3,2,1,0:T(8,128)S(1)}, f32[1,2,5,32,512]{4,3,2,1,0:T(8,128)}, u32[]{:S(2)}, u32[]{:S(2)}) collective-permute-start(f32[1,2,5,32,512]{4,3,2,1,0:T(8,128)S(1)} %maximum_bitcast_fusion), channel_id=1, source_target_pairs={{0,4},{4,8},{8,12},{12,16},{16,20},{20,24},{24,28},{1,5},{5,9},{9,... | collective-permute-start | bytes 1966088 | tf_op jit(solution)/shard_map/ppermute | solution.py:35
  204.4 37.8 %copy-start.5 = (f32[1,32,32,516]{3,2,0,1:T(8,128)S(1)}, f32[1,32,32,516]{3,2,0,1:T(8,128)}, u32[]{:S(2)}) copy-start(f32[1,32,32,516]{3,2,0,1:T(8,128)} %get-tuple-element.8) | copy-start | bytes 6340612
  237.2 13.5 %collective-permute-start.7 = (f32[1,2,5,32,512]{4,3,2,1,0:T(8,128)S(1)}, f32[1,2,5,32,512]{4,3,2,1,0:T(8,128)S(1)}, u32[]{:S(2)}, u32[]{:S(2)}) collective-permute-start(f32[1,2,5,32,512]{4,3,2,1,0:T(8,128)S(1)} %maximum_bitcast_fusion.1), channel_id=1, source_target_pairs={{1,0},{2,1},{3,2},{5,4},{6,5},{7,6},{9,8},{10,9},{11,10},{13,12},{... | collective-permute-start | bytes 1966088 | tf_op jit(solution)/shard_map/ppermute | solution.py:35
  238.5 12.2 %collective-permute-start.6 = (f32[1,2,5,32,512]{4,3,2,1,0:T(8,128)S(1)}, f32[1,2,5,32,512]{4,3,2,1,0:T(8,128)S(1)}, u32[]{:S(2)}, u32[]{:S(2)}) collective-permute-start(f32[1,2,5,32,512]{4,3,2,1,0:T(8,128)S(1)} %maximum_bitcast_fusion.1), channel_id=1, source_target_pairs={{0,1},{1,2},{2,3},{4,5},{5,6},{6,7},{8,9},{9,10},{10,11},{12,13},{... | collective-permute-start | bytes 1966088 | tf_op jit(solution)/shard_map/ppermute | solution.py:35
  246.1 5.5 %copy-start.3 = (f32[32,32,512]{2,1,0:T(8,128)S(1)}, f32[32,32,512]{2,1,0:T(8,128)}, u32[]{:S(2)}) copy-start(f32[32,32,512]{2,1,0:T(8,128)} %param.8) | copy-start | bytes 6291460
where the time goes:
time: 318 us; the launch traced here: 313 us
  other arithmetic  108 us (34%)
  matrix products  97.3 us (31%)
  local copies, waits for them, and re-layouts  58.8 us (18%)
  starting transfers between devices  29.5 us (9%)
  waiting for transfers between devices  14.1 us (4%)
  between operations  5.26 us (2%)
    dot_general x1, matrix products, local(): jnp.dot(right_z.reshape(-1, cells_z), local_inverse(cells_z), precision=h...  50.6 us
    dot_general x1, matrix products, local(): jnp.einsum('ij,fxjz->fxiz', block_inverse, right_y, precision=highest)  29.5 us
    select_n x2, other arithmetic, edge_flux(): return jnp.where(valid, fluxes(safe, direction), 0.0)  22.8 us
    unnamed x10, other arithmetic  20.3 us
    dot_general x1, matrix products, local(): jnp.einsum('ij,fjyz->fiyz', block_inverse, right_x, precision=highest)  17.2 us
    add x1, other arithmetic, stencil(): 0.5 * a_coef * (window(3) - window(1))  15.6 us
    dot_general x1, local copies, waits for them, and re-layouts, local(): jnp.einsum('ij,fjyz->fiyz', block_inverse, right_x, precision=highest)  14.3 us
    all_to_all x1, waiting for transfers between devices, local(): lax.all_to_all(paired, 'gx', split_axis=0, concat_axis=0, tiled=True)  14.1 us
  transfers between devices with their start and end apart: 9, of which 1 were waited for; matrix products, arithmetic and copies ran while one was open for 54% of the time, Pallas kernels for 0%

commit v1 on v0

v1 whole, which is shorter than its diff:
```python
import functools

import jax
import jax.numpy as jnp
import numpy as np
from jax import lax
from jax.experimental import pallas as pl
from jax.experimental.pallas import tpu as pltpu
from jax.sharding import PartitionSpec as P

beta_coef = 1.0 / 3.0
near_coef = 7.0 / 9.0
far_coef = 1.0 / 36.0
time_step = 0.4
highest = lax.Precision.HIGHEST
vmem_bytes = 50 * 1024 * 1024


def line_matrices(length):
    matrix = np.eye(length) + beta_coef * (np.eye(length, k=1) + np.eye(length, k=-1))
    rows = np.arange(length)
    spread = np.zeros((length, length + 4))
    spread[rows, rows + 3] += near_coef
    spread[rows, rows + 1] -= near_coef
    spread[rows, rows + 4] += far_coef
    spread[rows, rows] -= far_coef
    return np.linalg.inv(matrix), spread


def split_table(table):
    table = np.asarray(table, np.float32)
    high = table.astype(jnp.bfloat16)
    return high, (table - high.astype(np.float32)).astype(jnp.bfloat16)


def block_tables(cells, groups):
    length = cells * groups
    inverse, spread = line_matrices(length)
    whole = -time_step * inverse @ spread[:, 2:-2]
    own = np.zeros((groups, cells, cells))
    beyond = np.zeros((groups, 4, cells))
    act = np.zeros((groups, 4, cells))
    for g in range(groups):
        s, e = g * cells, (g + 1) * cells
        own[g] = whole[s:e, s:e]
        if g > 0:
            beyond[g, 0] = whole[s - 1, s:e]
            beyond[g, 1] = whole[s - 2, s:e]
            act[g, 0, 0] = 1.0
            act[g, 1, 1:] = inverse[s + 1 : e, s] / inverse[s + 1, s]
        if g < groups - 1:
            beyond[g, 2] = whole[e, s:e]
            beyond[g, 3] = whole[e + 1, s:e]
            act[g, 2, cells - 1] = 1.0
            act[g, 3, : cells - 1] = inverse[s : e - 1, e - 1] / inverse[e - 2, e - 1]
    return own, beyond, act


def edge_scalars(beyond, cells):
    groups = beyond.shape[0]
    table = np.zeros((groups, 2 * cells + 4))
    table[:, :cells] = beyond[:, 1]
    table[:, cells : 2 * cells] = beyond[:, 3]
    for g in range(groups):
        if g > 0:
            table[g, 2 * cells] = beyond[g, 0, 1] / beyond[g, 1, 1]
            table[g, 2 * cells + 1] = beyond[g, 0, 0] - table[g, 2 * cells] * beyond[g, 1, 0]
        if g < groups - 1:
            table[g, 2 * cells + 2] = beyond[g, 2, cells - 2] / beyond[g, 3, cells - 2]
            table[g, 2 * cells + 3] = (
                beyond[g, 2, cells - 1] - table[g, 2 * cells + 2] * beyond[g, 3, cells - 1]
            )
    return table


def common(fields):
    rho, m1, m2, m3, energy = fields
    inv = 1.0 / rho
    pressure = 0.4 * (energy - 0.5 * inv * (m1 * m1 + m2 * m2 + m3 * m3))
    return inv, pressure, energy + pressure


def flux_from(fields, shared, direction):
    inv, pressure, total = shared
    velocity = fields[1 + direction] * inv
    out = [fields[1 + direction]]
    for component in range(3):
        term = fields[1 + component] * velocity
        out.append(term + pressure if component == direction else term)
    out.append(total * velocity)
    return out


def load_fields(rho, mom, ene, idx):
    return [rho[idx], mom[(0,) + idx], mom[(1,) + idx], mom[(2,) + idx], ene[idx]]


def store_split(high_ref, low_ref, idx, value):
    high = value.astype(jnp.bfloat16)
    high_ref[idx] = high
    low_ref[idx] = (value - high.astype(jnp.float32)).astype(jnp.bfloat16)


def dot3(left_hi, left_lo, right_hi, right_lo):
    dot = functools.partial(jnp.dot, preferred_element_type=jnp.float32)
    return dot(left_hi, right_hi) + dot(left_lo, right_hi) + dot(left_hi, right_lo)


def edge_kernel(
    place, cx, ey_hi, ey_lo, rho, mom, ene, xlo, xhi, ylo, yhi, g_hi, g_lo, *, cells, tile, last
):
    step = pl.program_id(0)
    px = place[0]
    zs = rho.shape[2] // 128
    pieces = cells // 16

    @pl.when(step == 0)
    def _():
        xlo[...] = jnp.zeros_like(xlo)
        xhi[...] = jnp.zeros_like(xhi)

    def piece(n, _):
        yy = pl.multiple_of((n // zs) * 16, 16)
        zz = pl.multiple_of((n % zs) * 128, 128)
        ys, zc = pl.ds(yy, 16), pl.ds(zz, 128)
        low = [xlo[f, 1, ys, zc] for f in range(5)]
        high = [xhi[f, 1, ys, zc] for f in range(5)]
        first = end = None
        for x in range(tile):
            fields = load_fields(rho, mom, ene, (x, ys, zc))
            shared = common(fields)
            flux = flux_from(fields, shared, 0)
            if x == 0:
                first = flux
            end = flux
            cl = cx[px, step * tile + x]
            ch = cx[px, cells + step * tile + x]
            for f in range(5):
                low[f] += cl * flux[f]
                high[f] += ch * flux[f]
            side = flux_from(fields, shared, 1)
            rows = pl.ds(pl.multiple_of(x * cells + yy, 16), 16)
            for f in range(5):
                store_split(g_hi, g_lo, (f, rows, zc), side[f])
        for f in range(5):
            xlo[f, 1, ys, zc] = low[f]
            xhi[f, 1, ys, zc] = high[f]

        @pl.when(step == 0)
        def _():
            for f in range(5):
                xlo[f, 0, ys, zc] = cx[px, 2 * cells + 1] * first[f]

        @pl.when(step == last)
        def _():
            for f in range(5):
                xlo[f, 0, ys, zc] += cx[px, 2 * cells] * low[f]
                xhi[f, 0, ys, zc] = cx[px, 2 * cells + 2] * high[f] + cx[px, 2 * cells + 3] * end[f]

        return 0

    lax.fori_loop(0, pieces * zs, piece, 0)
    for f in range(5):
        got = dot3(ey_hi[0], ey_lo[0], g_hi[f], g_lo[f])
        for e in range(2):
            ylo[f, e] = got[e * tile : (e + 1) * tile]
            yhi[f, e] = got[(2 + e) * tile : (3 + e) * tile]


def xline_kernel(place, mx_hi, mx_lo, rho, mom, ene, out, f_hi, f_lo, *, cells):
    zs = rho.shape[2] // 128
    half = cells // 4

    def piece(n, _):
        xx = (n // zs) * 4
        zc = pl.ds(pl.multiple_of((n % zs) * 128, 128), 128)
        fields = [v.reshape(32, 128) for v in load_fields(rho, mom, ene, (pl.ds(xx, 4), slice(None), zc))]
        flux = flux_from(fields, common(fields), 0)
        rows = pl.ds(pl.multiple_of(xx * 8, 32), 32)
        for f in range(5):
            store_split(f_hi, f_lo, (f, rows, zc), flux[f])
        return 0

    lax.fori_loop(0, half * zs, piece, 0)
    for f in range(5):
        got = dot3(mx_hi[0], mx_lo[0], f_hi[f], f_lo[f]).reshape(cells, 8, -1)
        base = rho[...] if f == 0 else ene[...] if f == 4 else mom[f - 1]
        out[f] = base + got


def yz_kernel(
    place, my_hi, my_lo, mz_hi, mz_lo, wz, hg, rho, mom, ene, acc, out, g_hi, g_lo, h_hi, h_lo, *, cells, tile
):
    zs = rho.shape[2] // 128

    def piece(n, _):
        x = n // zs
        zc = pl.ds(pl.multiple_of((n % zs) * 128, 128), 128)
        fields = load_fields(rho, mom, ene, (x, slice(None), zc))
        shared = common(fields)
        rows = pl.ds(pl.multiple_of(x * cells, 32), cells)
        for direction, hi, lo in ((1, g_hi, g_lo), (2, h_hi, h_lo)):
            flux = flux_from(fields, shared, direction)
            for f in range(5):
                store_split(hi, lo, (f, rows, zc), flux[f])
        return 0

    lax.fori_loop(0, tile * zs, piece, 0)
    for f in range(5):
        ends = lax.dot_general(
            hg[f], wz[...], (((0,), (0,)), ((), ())), precision=highest,
            preferred_element_type=jnp.float32,
        )
        got = (
            dot3(my_hi[0], my_lo[0], g_hi[f], g_lo[f])
            + dot3(h_hi[f], h_lo[f], mz_hi[...], mz_lo[...])
            + ends
        )
        out[f] = acc[f] + got.reshape(tile, cells, -1)


def join_kernel(place, ax, ay, acc, xlo, xhi, ylo, yhi, out, *, cells, tile):
    step = pl.program_id(0)
    px = place[0]
    zs = acc.shape[3] // 128

    def piece(n, _):
        zc = pl.ds(pl.multiple_of(n * 128, 128), 128)
        for x in range(tile):
            i = step * tile + x
            at_low = jnp.where(i == 0, 0, 1)
            at_high = jnp.where(i == cells - 1, 0, 1)
            cl, ch = ax[px, i], ax[px, cells + i]
            for f in range(5):
                term = acc[f, x, :, zc] + cl * xlo[f, at_low, :, zc] + ch * xhi[f, at_high, :, zc]
                for e in range(2):
                    term += ay[0, e] * ylo[f, e, x : x + 1, zc] + ay[0, 2 + e] * yhi[f, e, x : x + 1, zc]
                out[f, x, :, zc] = term
        return 0

    lax.fori_loop(0, zs, piece, 0)


def ghost_fluxes(coarse_rows, ghost_rows, time_index, groups_x, place_x, cells):
    slots = ghost_rows.shape[2]
    capacity = slots // groups_x
    block = coarse_rows.shape[1]
    rows = ghost_rows[0]
    weights = time_index[0].astype(jnp.float32) * 0.125
    mine = (rows // block == place_x).astype(jnp.int32)
    upper = (np.arange(slots)[:, None] <= np.arange(slots)[None, :]).astype(np.float32)
    rank = jnp.dot(mine.astype(jnp.float32), upper, precision=highest).astype(jnp.int32) - 1
    wanted = jnp.arange(capacity, dtype=jnp.int32)
    pick = (mine[:, None, :] > 0) & (rank[:, None, :] == wanted[None, :, None])
    local_rows = jnp.sum(jnp.where(pick, (rows - place_x * block)[:, None, :], 0), axis=2).reshape(-1)
    level = jnp.sum(jnp.where(pick, weights[:, None, :], 0.0), axis=2).reshape(-1, 1)
    onehot = (local_rows[:, None] == jnp.arange(block)[None, :]).astype(jnp.float32)
    old = jnp.dot(onehot, coarse_rows[0, :, 0, :], precision=highest)
    new = jnp.dot(onehot, coarse_rows[1, :, 0, :], precision=highest)
    sent = ((1.0 - level) * old + level * new).reshape(groups_x, capacity, -1)
    got = lax.all_to_all(sent, "gx", split_axis=0, concat_axis=0, tiled=True).reshape(slots, -1)
    owner = lax.dynamic_index_in_dim(rows, place_x, 0, keepdims=False) // block
    earlier = np.arange(slots)[None, :] < np.arange(slots)[:, None]
    nth = jnp.sum(((owner[:, None] == owner[None, :]) & earlier).astype(jnp.int32), axis=1)
    back = ((owner * capacity + nth)[:, None] == jnp.arange(slots)[None, :]).astype(jnp.float32)
    ghosts = jnp.dot(back, got, precision=highest).reshape(4, cells, 5, cells)
    fields = [ghosts[:, :, f] for f in range(5)]
    flux = jnp.stack(flux_from(fields, common(fields), 2)).reshape(5, 4, cells * cells)
    return jnp.pad(flux, ((0, 0), (0, 4), (0, 0)))


def local(density, momentum, energy, coarse_rows, ghost_rows, time_index):
    cells, _, cells_z = density.shape
    groups_x, groups_y = lax.axis_size("gx"), lax.axis_size("gy")
    place_x, place_y = lax.axis_index("gx"), lax.axis_index("gy")
    place = jnp.stack([place_x, place_y]).astype(jnp.int32)
    tile = 8
    steps = cells // tile
    f32 = jnp.float32

    own_x, beyond_x, act_x = block_tables(cells, groups_x)
    own_y, beyond_y, act_y = block_tables(cells, groups_y)
    inverse_z, spread_z = line_matrices(cells_z)
    whole_z = -time_step * inverse_z @ spread_z
    mx = split_table(np.stack([np.kron(m, np.eye(8)) for m in own_x]))
    my = split_table(np.stack([np.kron(np.eye(tile), m) for m in own_y]))
    ey = split_table(
        np.stack(
            [np.einsum("ej,xk->exkj", m, np.eye(tile)).reshape(4 * tile, tile * cells) for m in beyond_y]
        )
    )
    mz = split_table(whole_z[:, 2:-2].T)
    wz = np.zeros((8, cells_z), np.float32)
    wz[:4] = whole_z[:, [0, 1, cells_z + 2, cells_z + 3]].T
    cx = edge_scalars(beyond_x, cells).astype(np.float32)
    ax = np.concatenate([act_x[:, 0] + act_x[:, 1], act_x[:, 2] + act_x[:, 3]], axis=1).astype(np.float32)
    ay = np.broadcast_to(act_y[..., None], act_y.shape + (128,)).astype(np.float32)

    hg = ghost_fluxes(coarse_rows, ghost_rows, time_index, groups_x, place_x, cells)

    smem = pl.BlockSpec(memory_space=pltpu.SMEM)
    xtile3 = pl.BlockSpec((tile, cells, cells_z), lambda i, p: (i, 0, 0))
    xtile4 = pl.BlockSpec((3, tile, cells, cells_z), lambda i, p: (0, i, 0, 0))
    xtile5 = pl.BlockSpec((5, tile, cells, cells_z), lambda i, p: (0, i, 0, 0))
    xplane = pl.BlockSpec((5, 2, cells, cells_z), lambda i, p: (0, 0, 0, 0))
    yplane = pl.BlockSpec((5, 2, tile, cells_z), lambda i, p: (0, 0, i, 0))
    params = pltpu.CompilerParams(vmem_limit_bytes=vmem_bytes, dimension_semantics=("arbitrary",))
    planes = jax.ShapeDtypeStruct((5, 2, cells, cells_z), f32)
    whole = jax.ShapeDtypeStruct((5, cells, cells, cells_z), f32)

    def fixed(table, which=None):
        dims = table.shape[1:]
        if which is None:
            return pl.BlockSpec(table.shape, lambda i, p: (0,) * table.ndim)
        return pl.BlockSpec((1,) + dims, lambda i, p: (p[which],) + (0,) * len(dims))

    def call(kernel, in_specs, out_shape, out_specs, scratch, cost, **more):
        return pl.pallas_call(
            kernel,
            grid_spec=pltpu.PrefetchScalarGridSpec(
                num_scalar_prefetch=1, grid=(steps,), in_specs=in_specs, out_specs=out_specs,
                scratch_shapes=scratch,
            ),
            out_shape=out_shape,
            compiler_params=params,
            cost_estimate=pl.CostEstimate(flops=cost[0], bytes_accessed=cost[1], transcendentals=0),
            **more,
        )

    size = 4 * 5 * cells * cells * cells_z
    rows = tile * cells
    half = pltpu.VMEM((5, rows, cells_z), jnp.bfloat16)
    xlo, xhi, ylo, yhi = call(
        functools.partial(edge_kernel, cells=cells, tile=tile, last=steps - 1),
        [smem, fixed(ey[0], 1), fixed(ey[1], 1), xtile3, xtile4, xtile3],
        [planes] * 4,
        [xplane, xplane, yplane, yplane],
        [half, half],
        (size * 20, size),
        name="edges",
    )(place, cx, *ey, density, momentum, energy)

    def shift(array, axis, by):
        peers = lax.axis_size(axis)
        return lax.ppermute(
            array, axis, [(i, i + by) for i in range(peers) if 0 <= i + by < peers]
        )

    in_xlo = shift(xhi, "gx", 1)
    in_xhi = shift(xlo, "gx", -1)
    in_ylo = shift(yhi, "gy", 1)
    in_yhi = shift(ylo, "gy", -1)

    ytile3 = pl.BlockSpec((cells, 8, cells_z), lambda i, p: (0, i, 0))
    ytile4 = pl.BlockSpec((3, cells, 8, cells_z), lambda i, p: (0, 0, i, 0))
    ytile5 = pl.BlockSpec((5, cells, 8, cells_z), lambda i, p: (0, 0, i, 0))
    acc = call(
        functools.partial(xline_kernel, cells=cells),
        [fixed(mx[0], 0), fixed(mx[1], 0), ytile3, ytile4, ytile3],
        whole,
        ytile5,
        [half, half],
        (size * 400, 2 * size),
        name="xlines",
    )(place, *mx, density, momentum, energy)
    acc = call(
        functools.partial(yz_kernel, cells=cells, tile=tile),
        [
            fixed(my[0], 1), fixed(my[1], 1), fixed(mz[0]), fixed(mz[1]), fixed(wz),
            pl.BlockSpec((5, 8, rows), lambda i, p: (0, 0, i)), xtile3, xtile4, xtile3, xtile5,
        ],
        whole,
        xtile5,
        [half] * 4,
        (size * 1200, 3 * size),
        name="yzlines",
    )(place, *my, *mz, wz, hg, density, momentum, energy, acc)
    return call(
        functools.partial(join_kernel, cells=cells, tile=tile),
        [smem, fixed(ay, 1), xtile5, xplane, xplane, yplane, yplane],
        whole,
        xtile5,
        [],
        (size * 4, 2 * size),
        name="join",
    )(place, ax, ay, acc, in_xlo, in_xhi, in_ylo, in_yhi)


def solution(mesh):
    return jax.shard_map(
        local,
        mesh=mesh,
        in_specs=(
            P("gx", "gy", None),
            P(None, "gx", "gy", None),
            P("gx", "gy", None),
            P(None, "gx", "gy", None),
            P("gy", None, None),
            P("gy", None, None),
        ),
        out_specs=P(None, "gx", "gy", None),
        check_vma=False,
    )
```

time: 318 us -> 108 us (0.34)
  the two profiles are of different devices: /device:TPU:0 before, /device:TPU:9 now
where the time goes in v1:
time: 108 us; the launch traced here: 107 us
  Pallas kernels  70.9 us (66%)
  starting transfers between devices  18.6 us (17%)
  local copies, waits for them, and re-layouts  9.85 us (9%)
  matrix products  3.81 us (4%)
  other arithmetic  3.65 us (3%)
    pallas_call x1, Pallas kernels, local(): call(functools.partial(yz_kernel, cells=cells, tile=tile), [fixed(my[0],...  32.4 us
    pallas_call x1, Pallas kernels, local(): call(functools.partial(xline_kernel, cells=cells), [fixed(mx[0], 0), fixe...  13.5 us
    pallas_call x1, Pallas kernels, local(): call(functools.partial(edge_kernel, cells=cells, tile=tile, last=steps -...  13.2 us
    ppermute x4, starting transfers between devices, shift(): lax.ppermute(array, axis, [(i, i + by) for i in range(peers) if 0 <= i +...  12.9 us
    pallas_call x1, Pallas kernels, local(): call(functools.partial(join_kernel, cells=cells, tile=tile), [smem, fixed...  11.7 us
    unnamed x27, local copies, waits for them, and re-layouts  6.56 us
    all_to_all x1, starting transfers between devices, ghost_fluxes(): lax.all_to_all(sent, 'gx', split_axis=0, concat_axis=0, tiled=True)  5.72 us
  transfers between devices with their start and end apart: 5, of which 0 were waited for; matrix products, arithmetic and copies ran while one was open for 4% of the time, Pallas kernels for 55%

profile of v1, /device:TPU:9, one launch (start us, length us, event | category | flops | bytes accessed | tf_op | source)
XLA Modules:
  0.0 107.0 jit_solution(3904414976303895450)
XLA Ops:
  0.0 0.8 convert_compare_fusion
  0.9 0.7 bitcast_subtract_fusion
  1.5 1.0 fusion.1
  2.5 0.2 select_reduce_fusion
  2.8 0.1 eq.92
  2.8 0.7 multiply_bitcast_fusion
  3.6 0.1 select_reduce_fusion.1
  3.6 0.1 reshape.344
  3.7 1.2 %convolution_multiply_fusion.1 = f32[128,160]{0,1:T(8,128)S(1)} fusion(f32[2,256,1,160]{1,3,2,0:T(8,128)} %param.23, s32[128]{0:T(128)S(1)} %eq.92, f32[128]{0:T(128)S(1)} %broadcast_subtract_fusion), kind=kOutput, calls=%fused_computation.2 | convolution fusion | flops 62967808 | bytes 246784 | tf_op jit(solution)/shard_map/dot_general | solution.py:258
  5.0 1.2 %fusion = f32[128,160]{0,1:T(8,128)S(1)} fusion(f32[128,160]{0,1:T(8,128)S(1)} %convolution_multiply_fusion.1, f32[2,256,1,160]{1,3,2,0:T(8,128)} %param.23, s32[128]{0:T(128)S(1)} %eq.92, f32[128]{0:T(128)S(1)} %reshape.344), kind=kOutput, calls=%fused_computation.1 | convolution fusion | flops 62988288 | bytes 328704 | tf_op jit(solution)/shard_map/dot_general | solution.py:259
  6.2 0.8 copy.23
  7.0 5.7 %all-to-all-start = ((f32[8,16,160]{2,1,0:T(8,128)}), f32[8,16,160]{2,1,0:T(8,128)}, u32[]{:S(2)}, u32[]{:S(2)}) async-start(f32[8,16,160]{2,1,0:T(8,128)} %bitcast.10), calls=%async_computation | async-start | bytes 262144 | tf_op jit(solution)/shard_map/all_to_all | solution.py:261
  12.7 0.1 pad_add_fusion.place
  12.8 0.8 copy-done.3
  13.6 0.8 copy-done.4
  14.4 0.7 copy-done.5
  15.1 13.2 %edges.1 = (f32[5,2,32,512]{3,2,1,0:T(8,128)}, f32[5,2,32,512]{3,2,1,0:T(8,128)}, f32[5,2,32,512]{3,2,1,0:T(8,128)}, f32[5,2,32,512]{3,2,1,0:T(8,128)}) custom-call(s32[2]{0:T(128)S(1)} %pad_add_fusion.place, f32[8,68]{1,0:T(8,128)S(1)} %copy-done.5, bf16[4,32,256]{2,1,0:T(8,128)(2,1)S(1)} %copy-done.3, bf16[4,32,256]{2,1,0:T(8,128)(2,1)S(1)} %copy-done.4, ...), custom_call_target="tpu_custom_call" | custom-call | flops 209715200 | bytes 10485760 | tf_op jit(solution)/shard_map/edges/pallas_call | solution.py:333
  28.4 3.1 %collective-permute-start = (f32[5,2,32,512]{3,2,1,0:T(8,128)}, f32[5,2,32,512]{3,2,1,0:T(8,128)S(1)}, u32[]{:S(2)}, u32[]{:S(2)}) collective-permute-start(f32[5,2,32,512]{3,2,1,0:T(8,128)} %get-tuple-element.9), channel_id=1, source_target_pairs={{0,4},{4,8},{8,12},{12,16},{16,20},{20,24},{24,28},{1,5},{5,9},{9,... | collective-permute-start | bytes 1966088 | tf_op jit(solution)/shard_map/ppermute | solution.py:345
  31.5 3.1 %collective-permute-start.1 = (f32[5,2,32,512]{3,2,1,0:T(8,128)}, f32[5,2,32,512]{3,2,1,0:T(8,128)S(1)}, u32[]{:S(2)}, u32[]{:S(2)}) collective-permute-start(f32[5,2,32,512]{3,2,1,0:T(8,128)} %get-tuple-element.10), channel_id=1, source_target_pairs={{4,0},{8,4},{12,8},{16,12},{20,16},{24,20},{28,24},{5,1},{9,5},{13... | collective-permute-start | bytes 1966088 | tf_op jit(solution)/shard_map/ppermute | solution.py:345
  34.6 4.8 %collective-permute-start.2 = (f32[5,2,32,512]{3,2,1,0:T(8,128)}, f32[5,2,32,512]{3,2,1,0:T(8,128)}, u32[]{:S(2)}, u32[]{:S(2)}) collective-permute-start(f32[5,2,32,512]{3,2,1,0:T(8,128)} %get-tuple-element.11), channel_id=1, source_target_pairs={{0,1},{1,2},{2,3},{4,5},{5,6},{6,7},{8,9},{9,10},{10,11},{12,13},{... | collective-permute-start | bytes 1966088 | tf_op jit(solution)/shard_map/ppermute | solution.py:345
  39.4 1.9 %collective-permute-start.3 = (f32[5,2,32,512]{3,2,1,0:T(8,128)}, f32[5,2,32,512]{3,2,1,0:T(8,128)}, u32[]{:S(2)}, u32[]{:S(2)}) collective-permute-start(f32[5,2,32,512]{3,2,1,0:T(8,128)} %get-tuple-element.12), channel_id=1, source_target_pairs={{1,0},{2,1},{3,2},{5,4},{6,5},{7,6},{9,8},{10,9},{11,10},{13,12},{... | collective-permute-start | bytes 1966088 | tf_op jit(solution)/shard_map/ppermute | solution.py:345
  41.3 0.7 and_select_fusion
  42.0 0.7 fusion.21
  42.7 0.2 convert_reduce_fusion
  42.9 0.1 reduce_sum.30
  43.0 0.1 squeeze.27
  43.1 0.0 copy-start.11
  43.1 13.5 %xlines.1.acc = f32[5,32,32,512]{3,2,1,0:T(8,128)} custom-call(s32[2]{0:T(128)S(1)} %pad_add_fusion.place, bf16[8,256,256]{2,1,0:T(8,128)(2,1)S(1)} %copy-done, bf16[8,256,256]{2,1,0:T(8,128)(2,1)S(1)} %copy-done.1, f32[32,32,512]{2,1,0:T(8,128)} %rho.5, f32[3,32,32,512]{3,2,1,0:T(8,128)} %mom.5, f32[32,32,512]{2,1,0:T(8,128)} %ene.5), custom_call_target="tpu_custom_call" | custom-call | flops 4194304000 | bytes 20971520 | tf_op jit(solution)/shard_map/xlines/pallas_call | solution.py:357
  56.6 0.0 all-to-all-done
  56.6 1.0 copy.24
  57.6 0.4 fusion.9
  58.1 0.1 stack.21
  58.2 0.1 div.78
  58.3 0.1 squeeze.32
  58.3 0.1 squeeze.33
  58.4 0.1 squeeze.34
  58.7 0.0 copy-start.7
  58.7 1.0 copy-done.7
  59.7 1.0 copy-done.8
  60.8 1.0 copy-done.9
  61.8 1.0 copy-done.10
  62.9 32.4 %yzlines.1.acc = f32[5,32,32,512]{3,2,1,0:T(8,128)} custom-call(s32[2]{0:T(128)S(1)} %pad_add_fusion.place, bf16[4,256,256]{2,1,0:T(8,128)(2,1)S(1)} %copy-done.7, bf16[4,256,256]{2,1,0:T(8,128)(2,1)S(1)} %copy-done.8, bf16[512,512]{1,0:T(8,128)(2,1)S(1)} %copy-done.9, bf16[512,512]{1,0:T(8,128)(2,1)S(1)} %copy-done.10, f32[8,512]{1,0:T(8,128)S(1)} %copy-done.11, ...), custom_call_target="tpu_custom_call" | custom-call | flops 12582912000 | bytes 31457280 | tf_op jit(solution)/shard_map/yzlines/pallas_call | solution.py:366
  95.2 0.0 collective-permute-done.xlo
  95.2 0.0 collective-permute-done.1.xhi
  95.2 0.0 collective-permute-done.2.ylo
  95.2 0.0 collective-permute-done.3.yhi
  95.2 0.0 copy-done.2
  95.3 11.7 %join.1 = f32[5,32,32,512]{3,2,1,0:T(8,128)} custom-call(s32[2]{0:T(128)S(1)} %pad_add_fusion.place, f32[8,64]{1,0:T(8,128)S(1)} %copy-done.6, f32[4,4,32,128]{3,2,1,0:T(8,128)S(1)} %copy-done.2, f32[5,32,32,512]{3,2,1,0:T(8,128)} %yzlines.1.acc, f32[5,2,32,512]{3,2,1,0:T(8,128)S(1)} %collective-permute-done.xlo, ...), custom_call_target="tpu_custom_call" | custom-call | flops 41943040 | bytes 20971520 | tf_op jit(solution)/shard_map/join/pallas_call | solution.py:378
  (25 shorter events, 0.2 us)
Async XLA Ops:
  0.0 43.1 %copy-start = (bf16[8,256,256]{2,1,0:T(8,128)(2,1)S(1)}, bf16[8,256,256]{2,1,0:T(8,128)(2,1)}, u32[]{:S(2)}) copy-start(bf16[8,256,256]{2,1,0:T(8,128)(2,1)} %constant.91.clone.mx_hi) | copy-start | bytes 3145732
  0.0 43.1 %copy-start.1 = (bf16[8,256,256]{2,1,0:T(8,128)(2,1)S(1)}, bf16[8,256,256]{2,1,0:T(8,128)(2,1)}, u32[]{:S(2)}) copy-start(bf16[8,256,256]{2,1,0:T(8,128)(2,1)} %constant.92.clone.mx_lo) | copy-start | bytes 3145732
  7.0 49.7 %all-to-all-start = ((f32[8,16,160]{2,1,0:T(8,128)}), f32[8,16,160]{2,1,0:T(8,128)}, u32[]{:S(2)}, u32[]{:S(2)}) async-start(f32[8,16,160]{2,1,0:T(8,128)} %bitcast.10), calls=%async_computation | async-start | bytes 262144 | tf_op jit(solution)/shard_map/all_to_all | solution.py:261
  12.8 0.8 copy-start.3
  13.6 0.8 copy-start.4
  14.4 0.7 copy-start.5
  15.1 27.6 %copy-start.12 = (pred[128,128]{1,0:T(32,128)(4,1)S(1)}, pred[128,128]{1,0:T(32,128)(4,1)}, u32[]{:S(2)}) copy-start(pred[128,128]{1,0:T(32,128)(4,1)} %constant.87.clone) | copy-start | bytes 49156
  28.4 66.8 %collective-permute-start = (f32[5,2,32,512]{3,2,1,0:T(8,128)}, f32[5,2,32,512]{3,2,1,0:T(8,128)S(1)}, u32[]{:S(2)}, u32[]{:S(2)}) collective-permute-start(f32[5,2,32,512]{3,2,1,0:T(8,128)} %get-tuple-element.9), channel_id=1, source_target_pairs={{0,4},{4,8},{8,12},{12,16},{16,20},{20,24},{24,28},{1,5},{5,9},{9,... | collective-permute-start | bytes 1966088 | tf_op jit(solution)/shard_map/ppermute | solution.py:345
  31.5 63.7 %collective-permute-start.1 = (f32[5,2,32,512]{3,2,1,0:T(8,128)}, f32[5,2,32,512]{3,2,1,0:T(8,128)S(1)}, u32[]{:S(2)}, u32[]{:S(2)}) collective-permute-start(f32[5,2,32,512]{3,2,1,0:T(8,128)} %get-tuple-element.10), channel_id=1, source_target_pairs={{4,0},{8,4},{12,8},{16,12},{20,16},{24,20},{28,24},{5,1},{9,5},{13... | collective-permute-start | bytes 1966088 | tf_op jit(solution)/shard_map/ppermute | solution.py:345
  34.6 60.7 %collective-permute-start.2 = (f32[5,2,32,512]{3,2,1,0:T(8,128)}, f32[5,2,32,512]{3,2,1,0:T(8,128)}, u32[]{:S(2)}, u32[]{:S(2)}) collective-permute-start(f32[5,2,32,512]{3,2,1,0:T(8,128)} %get-tuple-element.11), channel_id=1, source_target_pairs={{0,1},{1,2},{2,3},{4,5},{5,6},{6,7},{8,9},{9,10},{10,11},{12,13},{... | collective-permute-start | bytes 1966088 | tf_op jit(solution)/shard_map/ppermute | solution.py:345
  39.4 55.9 %collective-permute-start.3 = (f32[5,2,32,512]{3,2,1,0:T(8,128)}, f32[5,2,32,512]{3,2,1,0:T(8,128)}, u32[]{:S(2)}, u32[]{:S(2)}) collective-permute-start(f32[5,2,32,512]{3,2,1,0:T(8,128)} %get-tuple-element.12), channel_id=1, source_target_pairs={{1,0},{2,1},{3,2},{5,4},{6,5},{7,6},{9,8},{10,9},{11,10},{13,12},{... | collective-permute-start | bytes 1966088 | tf_op jit(solution)/shard_map/ppermute | solution.py:345
  43.1 15.6 %copy-start.11 = (f32[8,512]{1,0:T(8,128)S(1)}, f32[8,512]{1,0:T(8,128)}, u32[]{:S(2)}) copy-start(f32[8,512]{1,0:T(8,128)} %constant.97.clone.wz) | copy-start | bytes 49156
  58.7 1.0 copy-start.7
  59.7 1.0 copy-start.8
  60.8 1.0 copy-start.9
  61.8 1.0 copy-start.10
  62.8 32.4 %copy-start.2 = (f32[4,4,32,128]{3,2,1,0:T(8,128)S(1)}, f32[4,4,32,128]{3,2,1,0:T(8,128)}, u32[]{:S(2)}) copy-start(f32[4,4,32,128]{3,2,1,0:T(8,128)} %constant.99.clone.ay) | copy-start | bytes 786436
  62.8 32.4 %copy-start.6 = (f32[8,64]{1,0:T(8,128)S(1)}, f32[8,64]{1,0:T(8,128)}, u32[]{:S(2)}) copy-start(f32[8,64]{1,0:T(8,128)} %constant.98.clone.ax) | copy-start | bytes 6148

commit v2 on v1

v2 whole, which is shorter than its diff:
```python
import functools

import jax
import jax.numpy as jnp
import numpy as np
from jax import lax
from jax.experimental import pallas as pl
from jax.experimental.pallas import tpu as pltpu
from jax.sharding import PartitionSpec as P

beta_coef = 1.0 / 3.0
near_coef = 7.0 / 9.0
far_coef = 1.0 / 36.0
time_step = 0.4
highest = lax.Precision.HIGHEST
vmem_bytes = 50 * 1024 * 1024


def line_matrices(length):
    matrix = np.eye(length) + beta_coef * (np.eye(length, k=1) + np.eye(length, k=-1))
    rows = np.arange(length)
    spread = np.zeros((length, length + 4))
    spread[rows, rows + 3] += near_coef
    spread[rows, rows + 1] -= near_coef
    spread[rows, rows + 4] += far_coef
    spread[rows, rows] -= far_coef
    return np.linalg.inv(matrix), spread


def split_table(table):
    table = np.asarray(table, np.float32)
    high = table.astype(jnp.bfloat16).astype(np.float32)
    return high, (table - high).astype(jnp.bfloat16).astype(np.float32)


def scaled_rows(table, diagonal):
    rows, width = table.shape
    reach = np.clip(np.asarray(diagonal)[:, None] + np.arange(-14, 15)[None, :], -1, width)
    padded = np.concatenate([np.zeros((rows, 1)), table, np.zeros((rows, 1))], axis=1)
    near, which = np.unique(
        np.round(np.take_along_axis(padded, reach + 1, axis=1), 12), axis=0, return_inverse=True
    )
    scales = np.exp2(np.arange(4096) / 4096.0)
    best = np.zeros(near.shape[0])
    for i, row in enumerate(near):
        tried = row[None, :] / scales[:, None]
        error = tried.astype(np.float32).astype(jnp.bfloat16).astype(np.float64) - tried
        best[i] = scales[np.argmin(np.sum(np.square(error * scales[:, None]), axis=1))]
    scale = best[which.reshape(-1)].astype(np.float32).astype(np.float64)
    values = (table / scale[:, None]).astype(np.float32).astype(jnp.bfloat16)
    return scale, values.astype(np.float32)


def block_tables(cells, groups):
    length = cells * groups
    inverse, spread = line_matrices(length)
    whole = -time_step * inverse @ spread[:, 2:-2]
    own = np.zeros((groups, cells, cells))
    beyond = np.zeros((groups, 4, cells))
    act = np.zeros((groups, 4, cells))
    for g in range(groups):
        s, e = g * cells, (g + 1) * cells
        own[g] = whole[s:e, s:e]
        if g > 0:
            beyond[g, 0] = whole[s - 1, s:e]
            beyond[g, 1] = whole[s - 2, s:e]
            act[g, 0, 0] = 1.0
            act[g, 1, 1:] = inverse[s + 1 : e, s] / inverse[s + 1, s]
        if g < groups - 1:
            beyond[g, 2] = whole[e, s:e]
            beyond[g, 3] = whole[e + 1, s:e]
            act[g, 2, cells - 1] = 1.0
            act[g, 3, : cells - 1] = inverse[s : e - 1, e - 1] / inverse[e - 2, e - 1]
    return own, beyond, act


def edge_scalars(beyond, cells):
    groups = beyond.shape[0]
    table = np.zeros((groups, 2 * cells + 4))
    table[:, :cells] = beyond[:, 1]
    table[:, cells : 2 * cells] = beyond[:, 3]
    for g in range(groups):
        if g > 0:
            table[g, 2 * cells] = beyond[g, 0, 1] / beyond[g, 1, 1]
            table[g, 2 * cells + 1] = beyond[g, 0, 0] - table[g, 2 * cells] * beyond[g, 1, 0]
        if g < groups - 1:
            table[g, 2 * cells + 2] = beyond[g, 2, cells - 2] / beyond[g, 3, cells - 2]
            table[g, 2 * cells + 3] = (
                beyond[g, 2, cells - 1] - table[g, 2 * cells + 2] * beyond[g, 3, cells - 1]
            )
    return table


def common(fields):
    rho, m1, m2, m3, energy = fields
    inv = 1.0 / rho
    pressure = 0.4 * (energy - 0.5 * inv * (m1 * m1 + m2 * m2 + m3 * m3))
    return inv, pressure, energy + pressure


def flux_from(fields, shared, direction):
    inv, pressure, total = shared
    velocity = fields[1 + direction] * inv
    out = [fields[1 + direction]]
    for component in range(3):
        term = fields[1 + component] * velocity
        out.append(term + pressure if component == direction else term)
    out.append(total * velocity)
    return out


def load_fields(rho, mom, ene, idx):
    return [rho[idx], mom[(0,) + idx], mom[(1,) + idx], mom[(2,) + idx], ene[idx]]


def split(value):
    high = value.astype(jnp.bfloat16)
    return high, (value - high.astype(jnp.float32)).astype(jnp.bfloat16)


def edge_kernel(place, cx, cy, weights, rho, mom, ene, xlo, xhi, ylo, yhi, ysum, *, cells, tile, last):
    step = pl.program_id(0)
    px, py = place[0], place[1]
    zs = rho.shape[2] // 128

    @pl.when(step == 0)
    def _():
        xlo[...] = jnp.zeros_like(xlo)
        xhi[...] = jnp.zeros_like(xhi)

    def piece(n, _):
        zc = pl.ds(pl.multiple_of(n * 128, 128), 128)
        for yy in range(0, cells, 16):
            ys = pl.ds(yy, 16)
            low = [xlo[f, 1, ys, zc] for f in range(5)]
            high = [xhi[f, 1, ys, zc] for f in range(5)]
            for x in range(tile):
                fields = load_fields(rho, mom, ene, (x, ys, zc))
                shared = common(fields)
                flux = flux_from(fields, shared, 0)
                cl = cx[px, step * tile + x]
                ch = cx[px, cells + step * tile + x]
                for f in range(5):
                    low[f] += cl * flux[f]
                    high[f] += ch * flux[f]
                if x == 0:
                    first = flux

                    @pl.when(step == 0)
                    def _():
                        for f in range(5):
                            xlo[f, 0, ys, zc] = cx[px, 2 * cells + 1] * first[f]

                if x == tile - 1:
                    end = flux

                    @pl.when(step == last)
                    def _():
                        for f in range(5):
                            xhi[f, 0, ys, zc] = cx[px, 2 * cells + 3] * end[f]

                side = flux_from(fields, shared, 1)
                row = pl.ds(x, 1)
                for f in range(5):
                    for d, out in ((0, ylo), (1, yhi)):
                        part = side[f] * weights[0, d, ys]
                        part = part[:8] + part[8:]
                        if yy > 0:
                            part += ysum[f, d, x]
                        if yy + 16 < cells:
                            ysum[f, d, x] = part
                        else:
                            total = jnp.sum(part, axis=0, keepdims=True)
                            out[f, 1, row, zc] = total
                            if d == 0:
                                out[f, 0, row, zc] += cy[py, 2 * cells] * total
                            else:
                                out[f, 0, row, zc] = (
                                    cy[py, 2 * cells + 2] * total + cy[py, 2 * cells + 3] * side[f][15:]
                                )
                    if yy == 0:
                        ylo[f, 0, row, zc] = cy[py, 2 * cells + 1] * side[f][:1]
            for f in range(5):
                xlo[f, 1, ys, zc] = low[f]
                xhi[f, 1, ys, zc] = high[f]

            @pl.when(step == last)
            def _():
                for f in range(5):
                    xlo[f, 0, ys, zc] += cx[px, 2 * cells] * low[f]
                    xhi[f, 0, ys, zc] += cx[px, 2 * cells + 2] * high[f]

        return 0

    lax.fori_loop(0, zs, piece, 0)


def lines_kernel(
    place, mx, my, mz, wz, sx, sy, sz, hg, rho, mom, ene, out,
    f_buf, g_buf, h_buf, acc, mx_buf, my_buf, mz_buf, *, cells, tile, steps
):
    step = pl.program_id(0)
    width = rho.shape[2]
    zs = width // 128
    rows = tile * cells
    bf16 = jnp.bfloat16
    dot = functools.partial(jnp.dot, preferred_element_type=jnp.float32)
    chunks = [(z * 128, (z + 1) * 128) for z in range(zs)]

    @pl.when(step == 0)
    def _():
        for buf, table in ((mx_buf, mx[0]), (my_buf, my[0])):
            buf[:, :rows] = table.astype(bf16)
            buf[:, rows:] = table.astype(bf16)
        mz_buf[...] = mz[...].astype(bf16)

    @pl.when(step < steps)
    def _():
        def piece(n, _):
            x = (n // (2 * zs)) * 2
            yy = pl.multiple_of((n // zs) % 2 * 16, 16)
            zc = pl.multiple_of((n % zs) * 128, 128)
            z_hi, z_lo = pl.ds(zc, 128), pl.ds(width + zc, 128)
            fields = load_fields(rho, mom, ene, (pl.ds(x, 2), pl.ds(yy, 16), z_hi))
            shared = common(fields)
            for f, value in enumerate(flux_from(fields, shared, 0)):
                for j in range(2):
                    hi, lo = split(value[:, 8 * j : 8 * j + 8].reshape(16, 128))
                    at = pl.multiple_of((step * tile + x) * 8, 16)
                    f_buf[yy // 8 + j, f, pl.ds(at, 16), z_hi] = hi
                    f_buf[yy // 8 + j, f, pl.ds(cells * 8 + at, 16), z_hi] = lo
            for f, value in enumerate(flux_from(fields, shared, 1)):
                for j in range(2):
                    hi, lo = split(value[j])
                    at = pl.multiple_of((x + j) * cells + yy, 16)
                    g_buf[f, pl.ds(at, 16), z_hi] = hi
                    g_buf[f, pl.ds(rows + at, 16), z_hi] = lo
            for f, value in enumerate(flux_from(fields, shared, 2)):
                for j in range(2):
                    hi, lo = split(value[j])
                    at = pl.multiple_of((x + j) * cells + yy, 16)
                    h_buf[f, pl.ds(at, 16), z_hi] = hi
                    h_buf[f, pl.ds(at, 16), z_lo] = lo
            return 0

        lax.fori_loop(0, (tile // 2) * 2 * zs, piece, 0)
        half = width // 2
        for f in range(5):
            base = rho if f == 0 else ene if f == 4 else mom.at[f - 1]
            y_part = dot(my_buf[...], g_buf[f])
            g_hi, g_lo = split(hg[f])
            g_hi, g_lo = g_hi.astype(jnp.float32), g_lo.astype(jnp.float32)
            ghost = jnp.concatenate([g_hi, g_lo, g_hi], axis=0).astype(bf16)
            for k in range(2):
                low = 0 if k == 0 else half - 128
                high = half + 128 if k == 0 else width
                left = jnp.concatenate([h_buf[f, :, low:high], h_buf[f, :, width + low : width + high]], axis=1)
                weight = mz_buf[low:high, k * half : (k + 1) * half]
                z_part = dot(left, jnp.concatenate([weight, weight], axis=0))
                edge = slice(0, 128) if k == 0 else slice(width - 128, width)
                ends = lax.dot_general(
                    ghost, wz[:, edge].astype(bf16), (((0,), (0,)), ((), ())),
                    preferred_element_type=jnp.float32,
                )
                for a, b in chunks[k * zs // 2 : (k + 1) * zs // 2]:
                    got = z_part[:, a - k * half : b - k * half]
                    if a == edge.start:
                        got = got + ends
                    got = got * sz[:, a:b] + y_part[:, a:b] * sy[0]
                    acc[f, pl.ds(step * tile, tile), :, a:b] = base[:, :, a:b] + got.reshape(tile, cells, 128)

    @pl.when(step >= steps)
    def _():
        j = step - steps
        at = pl.multiple_of(j * 8, 8)
        for f in range(5):
            got = dot(mx_buf[...], f_buf[j, f])
            for a, b in chunks:
                part = (got[:, a:b] * sx[0]).reshape(cells, 8, 128)
                out[f, :, :, a:b] = acc[f, :, pl.ds(at, 8), a:b] + part


def join_kernel(place, ax, ay, acc, xlo, xhi, ylo, yhi, out, *, cells, tile):
    step = pl.program_id(0)
    px = place[0]
    zs = acc.shape[3] // 128

    def piece(n, _):
        zc = pl.ds(pl.multiple_of(n * 128, 128), 128)
        for x in range(tile):
            i = step * tile + x
            at_low = jnp.where(i == 0, 0, 1)
            at_high = jnp.where(i == cells - 1, 0, 1)
            cl, ch = ax[px, i], ax[px, cells + i]
            for f in range(5):
                y_low, y_high = ylo[f, 1, x : x + 1, zc], yhi[f, 1, x : x + 1, zc]
                for yy in range(0, cells, 8):
                    ys = slice(yy, yy + 8)
                    term = acc[f, x, ys, zc] + cl * xlo[f, at_low, ys, zc] + ch * xhi[f, at_high, ys, zc]
                    term += ay[0, 1, ys] * y_low + ay[0, 3, ys] * y_high
                    if yy == 0:
                        term += ay[0, 0, ys] * ylo[f, 0, x : x + 1, zc]
                    if yy + 8 == cells:
                        term += ay[0, 2, ys] * yhi[f, 0, x : x + 1, zc]
                    out[f, x, ys, zc] = term
        return 0

    lax.fori_loop(0, zs, piece, 0)


def ghost_fluxes(coarse_rows, ghost_rows, time_index, groups_x, place_x, cells):
    slots = ghost_rows.shape[2]
    capacity = slots // groups_x
    block = coarse_rows.shape[1]
    rows = ghost_rows[0]
    weights = time_index[0].astype(jnp.float32) * 0.125
    mine = (rows // block == place_x).astype(jnp.int32)
    upper = (np.arange(slots)[:, None] <= np.arange(slots)[None, :]).astype(np.float32)
    rank = jnp.dot(mine.astype(jnp.float32), upper, precision=highest).astype(jnp.int32) - 1
    wanted = jnp.arange(capacity, dtype=jnp.int32)
    pick = (mine[:, None, :] > 0) & (rank[:, None, :] == wanted[None, :, None])
    local_rows = jnp.sum(jnp.where(pick, (rows - place_x * block)[:, None, :], 0), axis=2).reshape(-1)
    level = jnp.sum(jnp.where(pick, weights[:, None, :], 0.0), axis=2).reshape(-1, 1)
    onehot = (local_rows[:, None] == jnp.arange(block)[None, :]).astype(jnp.float32)
    old = jnp.dot(onehot, coarse_rows[0, :, 0, :], precision=highest)
    new = jnp.dot(onehot, coarse_rows[1, :, 0, :], precision=highest)
    sent = ((1.0 - level) * old + level * new).reshape(groups_x, capacity, -1)
    every = lax.all_gather(sent, "gx")
    got = lax.dynamic_index_in_dim(every, place_x, 1, keepdims=False).reshape(slots, -1)
    owner = lax.dynamic_index_in_dim(rows, place_x, 0, keepdims=False) // block
    earlier = np.arange(slots)[None, :] < np.arange(slots)[:, None]
    nth = jnp.sum(((owner[:, None] == owner[None, :]) & earlier).astype(jnp.int32), axis=1)
    back = ((owner * capacity + nth)[:, None] == jnp.arange(slots)[None, :]).astype(jnp.float32)
    ghosts = jnp.dot(back, got, precision=highest).reshape(4, cells, 5, cells)
    fields = [ghosts[:, :, f] for f in range(5)]
    flux = jnp.stack(flux_from(fields, common(fields), 2)).reshape(5, 4, cells * cells)
    return jnp.pad(flux, ((0, 0), (0, 4), (0, 0)))


def local(density, momentum, energy, coarse_rows, ghost_rows, time_index):
    cells, _, cells_z = density.shape
    groups_x, groups_y = lax.axis_size("gx"), lax.axis_size("gy")
    place_x, place_y = lax.axis_index("gx"), lax.axis_index("gy")
    place = jnp.stack([place_x, place_y]).astype(jnp.int32)
    tile = 8
    steps = cells // tile
    f32 = jnp.float32

    own_x, beyond_x, act_x = block_tables(cells, groups_x)
    own_y, beyond_y, act_y = block_tables(cells, groups_y)
    inverse_z, spread_z = line_matrices(cells_z)
    whole_z = -time_step * inverse_z @ spread_z
    at_x = np.tile(np.arange(cells), groups_x)
    at_y = np.tile(np.arange(cells), groups_y)
    scale_x, values_x = scaled_rows(own_x.reshape(-1, cells), at_x)
    scale_y, values_y = scaled_rows(own_y.reshape(-1, cells), at_y)
    scale_z, values_z = scaled_rows(whole_z[:, 2:-2], np.arange(cells_z))
    lanes = np.ones((1, 128), np.float32)
    mx = np.stack([np.kron(m, np.eye(8)) for m in values_x.reshape(own_x.shape)]).astype(np.float32)
    my = np.stack([np.kron(np.eye(tile), m) for m in values_y.reshape(own_y.shape)]).astype(np.float32)
    mz = np.ascontiguousarray(values_z.T)
    sx = np.stack([np.repeat(v, 8)[:, None] * lanes for v in scale_x.reshape(groups_x, cells)])
    sy = np.stack([np.tile(v, tile)[:, None] * lanes for v in scale_y.reshape(groups_y, cells)])
    sx, sy, sz = sx.astype(np.float32), sy.astype(np.float32), scale_z[None, :].astype(np.float32)
    ends = np.zeros((8, cells_z), np.float32)
    ends[:4] = (whole_z[:, [0, 1, cells_z + 2, cells_z + 3]] / scale_z[:, None]).T
    ends_hi, ends_lo = split_table(ends)
    wz = np.concatenate([ends_hi, ends_hi, ends_lo])
    cy = edge_scalars(beyond_y, cells).astype(np.float32)
    weights = np.broadcast_to(beyond_y[:, 1::2, :, None], (groups_y, 2, cells, 128)).astype(np.float32)
    cx = edge_scalars(beyond_x, cells).astype(np.float32)
    ax = np.concatenate([act_x[:, 0] + act_x[:, 1], act_x[:, 2] + act_x[:, 3]], axis=1).astype(np.float32)
    ay = np.broadcast_to(act_y[..., None], act_y.shape + (128,)).astype(np.float32)

    hg = ghost_fluxes(coarse_rows, ghost_rows, time_index, groups_x, place_x, cells)

    smem = pl.BlockSpec(memory_space=pltpu.SMEM)
    xtile3 = pl.BlockSpec((tile, cells, cells_z), lambda i, p: (i, 0, 0))
    xtile4 = pl.BlockSpec((3, tile, cells, cells_z), lambda i, p: (0, i, 0, 0))
    xtile5 = pl.BlockSpec((5, tile, cells, cells_z), lambda i, p: (0, i, 0, 0))
    xplane = pl.BlockSpec((5, 2, cells, cells_z), lambda i, p: (0, 0, 0, 0))
    yplane = pl.BlockSpec((5, 2, tile, cells_z), lambda i, p: (0, 0, i, 0))
    params = pltpu.CompilerParams(vmem_limit_bytes=vmem_bytes, dimension_semantics=("arbitrary",))
    planes = jax.ShapeDtypeStruct((5, 2, cells, cells_z), f32)
    whole = jax.ShapeDtypeStruct((5, cells, cells, cells_z), f32)

    def fixed(table, which=None):
        dims = table.shape[1:]
        if which is None:
            return pl.BlockSpec(table.shape, lambda i, p: (0,) * table.ndim)
        return pl.BlockSpec((1,) + dims, lambda i, p: (p[which],) + (0,) * len(dims))

    def call(kernel, in_specs, out_shape, out_specs, scratch, cost, grid=steps, **more):
        return pl.pallas_call(
            kernel,
            grid_spec=pltpu.PrefetchScalarGridSpec(
                num_scalar_prefetch=1, grid=(grid,), in_specs=in_specs, out_specs=out_specs,
                scratch_shapes=scratch,
            ),
            out_shape=out_shape,
            compiler_params=params,
            cost_estimate=pl.CostEstimate(flops=cost[0], bytes_accessed=cost[1], transcendentals=0),
            **more,
        )

    size = 4 * 5 * cells * cells * cells_z
    rows = tile * cells
    bf16 = jnp.bfloat16
    xlo, xhi, ylo, yhi = call(
        functools.partial(edge_kernel, cells=cells, tile=tile, last=steps - 1),
        [smem, smem, fixed(weights, 1), xtile3, xtile4, xtile3],
        [planes] * 4,
        [xplane, xplane, yplane, yplane],
        [pltpu.VMEM((5, 2, tile, 8, 128), f32)],
        (size * 20, size),
        name="edges",
    )(place, cx, cy, weights, density, momentum, energy)

    def shift(array, axis, by):
        peers = lax.axis_size(axis)
        return lax.ppermute(
            array, axis, [(i, i + by) for i in range(peers) if 0 <= i + by < peers]
        )

    in_xlo = shift(xhi, "gx", 1)
    in_xhi = shift(xlo, "gx", -1)
    in_ylo = shift(yhi, "gy", 1)
    in_yhi = shift(ylo, "gy", -1)

    top = steps - 1
    acc = call(
        functools.partial(lines_kernel, cells=cells, tile=tile, steps=steps),
        [
            fixed(mx, 0), fixed(my, 1), fixed(mz), fixed(wz), fixed(sx, 0), fixed(sy, 1), fixed(sz),
            pl.BlockSpec((5, 8, rows), lambda i, p: (0, 0, jnp.minimum(i, top))),
            pl.BlockSpec((tile, cells, cells_z), lambda i, p: (jnp.minimum(i, top), 0, 0)),
            pl.BlockSpec((3, tile, cells, cells_z), lambda i, p: (0, jnp.minimum(i, top), 0, 0)),
            pl.BlockSpec((tile, cells, cells_z), lambda i, p: (jnp.minimum(i, top), 0, 0)),
        ],
        whole,
        pl.BlockSpec((5, cells, 8, cells_z), lambda i, p: (0, 0, jnp.maximum(i - steps, 0), 0)),
        [
            pltpu.VMEM((cells // 8, 5, 2 * cells * 8, cells_z), bf16),
            pltpu.VMEM((5, 2 * rows, cells_z), bf16),
            pltpu.VMEM((5, rows, 2 * cells_z), bf16),
            pltpu.VMEM((5, cells, cells, cells_z), f32),
            pltpu.VMEM((cells * 8, 2 * cells * 8), bf16),
            pltpu.VMEM((rows, 2 * rows), bf16),
            pltpu.VMEM((cells_z, cells_z), bf16),
        ],
        (size * 1200, 2 * size),
        grid=2 * steps,
        name="lines",
    )(place, mx, my, mz, wz, sx, sy, sz, hg, density, momentum, energy)
    return call(
        functools.partial(join_kernel, cells=cells, tile=tile),
        [smem, fixed(ay, 1), xtile5, xplane, xplane, yplane, yplane],
        whole,
        xtile5,
        [],
        (size * 4, 2 * size),
        name="join",
    )(place, ax, ay, acc, in_xlo, in_xhi, in_ylo, in_yhi)


def solution(mesh):
    return jax.shard_map(
        local,
        mesh=mesh,
        in_specs=(
            P("gx", "gy", None),
            P(None, "gx", "gy", None),
            P("gx", "gy", None),
            P(None, "gx", "gy", None),
            P("gy", None, None),
            P("gy", None, None),
        ),
        out_specs=P(None, "gx", "gy", None),
        check_vma=False,
    )
```

time: 108 us -> 126 us (1.17)
  the two profiles are of different devices: /device:TPU:9 before, /device:TPU:0 now
where the time goes in v2:
time: 126 us; the launch traced here: 125 us
  blocking collectives  50.8 us (40%)
  Pallas kernels  50.3 us (40%)
  local copies, waits for them, and re-layouts  10.6 us (8%)
  starting transfers between devices  8.99 us (7%)
  matrix products  2.98 us (2%)
  other arithmetic  1.43 us (1%)
    all_gather x1, blocking collectives, ghost_fluxes(): every = lax.all_gather(sent, 'gx')  50.8 us
    pallas_call x1, Pallas kernels, local(): call(functools.partial(lines_kernel, cells=cells, tile=tile, steps=steps)...  28 us
    pallas_call x1, Pallas kernels, local(): call(functools.partial(join_kernel, cells=cells, tile=tile), [smem, fixed...  11.4 us
    pallas_call x1, Pallas kernels, local(): call(functools.partial(edge_kernel, cells=cells, tile=tile, last=steps -...  10.9 us
    ppermute x4, starting transfers between devices, shift(): lax.ppermute(array, axis, [(i, i + by) for i in range(peers) if 0 <= i +...  8.99 us
    unnamed x31, local copies, waits for them, and re-layouts  7.01 us
  transfers between devices with their start and end apart: 4, of which 0 were waited for; matrix products, arithmetic and copies ran while one was open for 6% of the time, Pallas kernels for 22%

profile of v2, /device:TPU:0, one launch (start us, length us, event | category | flops | bytes accessed | tf_op | source)
XLA Modules:
  0.0 125.4 jit_solution(5311932254072395824)
XLA Ops:
  0.0 0.1 pad_add_fusion.place
  0.1 0.9 copy-done.1
  1.0 0.7 copy-done.2
  1.7 0.7 copy-done.4
  2.4 10.9 %edges.1 = (f32[5,2,32,512]{3,2,1,0:T(8,128)}, f32[5,2,32,512]{3,2,1,0:T(8,128)}, f32[5,2,32,512]{3,2,1,0:T(8,128)S(1)}, f32[5,2,32,512]{3,2,1,0:T(8,128)}) custom-call(s32[2]{0:T(128)S(1)} %pad_add_fusion.place, f32[8,68]{1,0:T(8,128)S(1)} %copy-done.2, f32[4,68]{1,0:T(4,128)S(1)} %copy-done.4, f32[4,2,32,128]{3,2,1,0:T(8,128)S(1)} %copy-done.1, ...), custom_call_target="tpu_custom_call" | custom-call | flops 209715200 | bytes 10485760 | tf_op jit(solution)/shard_map/edges/pallas_call | solution.py:409
  13.3 4.9 %collective-permute-start = (f32[5,2,32,512]{3,2,1,0:T(8,128)}, f32[5,2,32,512]{3,2,1,0:T(8,128)S(1)}, u32[]{:S(2)}, u32[]{:S(2)}) collective-permute-start(f32[5,2,32,512]{3,2,1,0:T(8,128)} %get-tuple-element.9), channel_id=1, source_target_pairs={{0,4},{4,8},{8,12},{12,16},{16,20},{20,24},{24,28},{1,5},{5,9},{9,... | collective-permute-start | bytes 1966088 | tf_op jit(solution)/shard_map/ppermute | solution.py:421
  18.2 1.3 %collective-permute-start.1 = (f32[5,2,32,512]{3,2,1,0:T(8,128)}, f32[5,2,32,512]{3,2,1,0:T(8,128)S(1)}, u32[]{:S(2)}, u32[]{:S(2)}) collective-permute-start(f32[5,2,32,512]{3,2,1,0:T(8,128)} %get-tuple-element.10), channel_id=1, source_target_pairs={{4,0},{8,4},{12,8},{16,12},{20,16},{24,20},{28,24},{5,1},{9,5},{13... | collective-permute-start | bytes 1966088 | tf_op jit(solution)/shard_map/ppermute | solution.py:421
  19.5 1.5 %collective-permute-start.2 = (f32[5,2,32,512]{3,2,1,0:T(8,128)}, f32[5,2,32,512]{3,2,1,0:T(8,128)S(1)}, u32[]{:S(2)}, u32[]{:S(2)}) collective-permute-start(f32[5,2,32,512]{3,2,1,0:T(8,128)} %get-tuple-element.11), channel_id=1, source_target_pairs={{0,1},{1,2},{2,3},{4,5},{5,6},{6,7},{8,9},{9,10},{10,11},{12,13},{... | collective-permute-start | bytes 1966088 | tf_op jit(solution)/shard_map/ppermute | solution.py:421
  21.0 1.3 %collective-permute-start.3 = (f32[5,2,32,512]{3,2,1,0:T(8,128)S(1)}, f32[5,2,32,512]{3,2,1,0:T(8,128)S(1)}, u32[]{:S(2)}, u32[]{:S(2)}) collective-permute-start(f32[5,2,32,512]{3,2,1,0:T(8,128)S(1)} %get-tuple-element.12), channel_id=1, source_target_pairs={{1,0},{2,1},{3,2},{5,4},{6,5},{7,6},{9,8},{10,9},{11,10},{13,12},{... | collective-permute-start | bytes 1966088 | tf_op jit(solution)/shard_map/ppermute | solution.py:421
  22.3 0.0 copy-done.13
  22.4 0.1 squeeze.29
  22.5 0.0 copy-done.12
  22.5 0.2 convert_reduce_fusion
  22.7 0.1 reduce_sum.30
  22.8 0.0 copy-done.11
  22.8 0.2 fusion.1
  22.9 0.2 select_reduce_fusion
  23.2 0.1 eq.92
  23.2 0.0 copy-done.14
  23.3 0.1 select_reduce_fusion.1
  23.4 0.1 reshape.342
  23.4 1.2 convolution_multiply_fusion.1
  24.7 1.2 fusion
  25.9 0.1 copy.25
  26.0 50.8 %all_gather.3 = f32[8,8,16,160]{3,2,1,0:T(8,128)S(1)} all-gather(f32[1,8,16,160]{3,2,1,0:T(8,128)S(1)} %bitcast.71), channel_id=1, replica_groups=mesh['gx'=8,'gy'=4] {'gx'}, dimensions={0}, use_global_device_ids=true | all-gather | bytes 737280 | tf_op jit(solution)/shard_map/all_gather | solution.py:328
  76.9 0.1 copy.26
  77.0 0.4 fusion.9
  77.4 0.7 fusion.23
  78.1 0.9 squeeze.36
  79.0 0.9 stack.21
  79.9 0.9 div.78
  80.9 0.1 squeeze.35
  81.0 0.1 squeeze.34
  81.2 0.0 copy-done.9
  81.2 0.0 copy-done.10
  81.2 0.0 copy-start.5
  81.2 1.2 copy-done.5
  82.4 1.2 copy-done.6
  83.7 1.2 copy-done.7
  84.9 1.0 copy-done.8
  85.9 28.0 %lines.1.acc = f32[5,32,32,512]{3,2,1,0:T(8,128)} custom-call(s32[2]{0:T(128)S(1)} %pad_add_fusion.place, f32[8,256,256]{2,1,0:T(8,128)} %constant.95.clone.mx, f32[4,256,256]{2,1,0:T(8,128)S(1)} %copy-done.7, f32[512,512]{1,0:T(8,128)S(1)} %copy-done.6, f32[24,512]{1,0:T(8,128)S(1)} %copy-done.9, f32[8,256,128]{2,1,0:T(8,128)S(1)} %copy-done.5, ...), custom_call_target="tpu_custom_call" | custom-call | flops 12582912000 | bytes 20971520 | tf_op jit(solution)/shard_map/lines/pallas_call | solution.py:431
  113.9 0.0 collective-permute-done.xlo
  113.9 0.0 collective-permute-done.1.xhi
  113.9 0.0 collective-permute-done.2.ylo
  113.9 0.0 collective-permute-done.3.yhi
  113.9 0.0 copy-done
  114.0 0.0 copy-done.3
  114.0 11.4 %join.1 = f32[5,32,32,512]{3,2,1,0:T(8,128)} custom-call(s32[2]{0:T(128)S(1)} %pad_add_fusion.place, f32[8,64]{1,0:T(8,128)S(1)} %copy-done.3, f32[4,4,32,128]{3,2,1,0:T(8,128)S(1)} %copy-done, f32[5,32,32,512]{3,2,1,0:T(8,128)} %lines.1.acc, f32[5,2,32,512]{3,2,1,0:T(8,128)S(1)} %collective-permute-done.xlo, ...), custom_call_target="tpu_custom_call" | custom-call | flops 41943040 | bytes 20971520 | tf_op jit(solution)/shard_map/join/pallas_call | solution.py:455
  (28 shorter events, 0.2 us)
Async XLA Ops:
  0.0 22.5 %copy-start.12 = (pred[128,128]{1,0:T(32,128)(4,1)S(1)}, pred[128,128]{1,0:T(32,128)(4,1)}, u32[]{:S(2)}) copy-start(pred[128,128]{1,0:T(32,128)(4,1)} %constant.91.clone) | copy-start | bytes 49156
  0.0 22.3 %copy-start.13 = (s32[1,8,128]{2,1,0:T(8,128)S(1)}, s32[1,8,128]{2,1,0:T(8,128)}, u32[]{:S(2)}) copy-start(s32[1,8,128]{2,1,0:T(8,128)} %param.24) | copy-start | bytes 12292
  0.0 23.2 %copy-start.14 = (s32[1,8,128]{2,1,0:T(8,128)S(1)}, s32[1,8,128]{2,1,0:T(8,128)}, u32[]{:S(2)}) copy-start(s32[1,8,128]{2,1,0:T(8,128)} %param.25) | copy-start | bytes 12292
  0.1 0.9 copy-start.1
  1.0 0.7 copy-start.2
  1.7 0.7 copy-start.4
  2.4 20.4 %copy-start.11 = (f32[128,128]{1,0:T(8,128)S(1)}, f32[128,128]{1,0:T(8,128)}, u32[]{:S(2)}) copy-start(f32[128,128]{1,0:T(8,128)} %constant.90.clone) | copy-start | bytes 196612
  2.4 78.8 %copy-start.9 = (f32[24,512]{1,0:T(8,128)S(1)}, f32[24,512]{1,0:T(8,128)}, u32[]{:S(2)}) copy-start(f32[24,512]{1,0:T(8,128)} %constant.98.clone.wz) | copy-start | bytes 147460
  2.4 78.8 %copy-start.10 = (f32[1,512]{1,0:T(1,128)S(1)}, f32[1,512]{1,0:T(1,128)}, u32[]{:S(2)}) copy-start(f32[1,512]{1,0:T(1,128)} %constant.101.clone.sz) | copy-start | bytes 6148
  13.3 100.6 %collective-permute-start = (f32[5,2,32,512]{3,2,1,0:T(8,128)}, f32[5,2,32,512]{3,2,1,0:T(8,128)S(1)}, u32[]{:S(2)}, u32[]{:S(2)}) collective-permute-start(f32[5,2,32,512]{3,2,1,0:T(8,128)} %get-tuple-element.9), channel_id=1, source_target_pairs={{0,4},{4,8},{8,12},{12,16},{16,20},{20,24},{24,28},{1,5},{5,9},{9,... | collective-permute-start | bytes 1966088 | tf_op jit(solution)/shard_map/ppermute | solution.py:421
  18.2 95.7 %collective-permute-start.1 = (f32[5,2,32,512]{3,2,1,0:T(8,128)}, f32[5,2,32,512]{3,2,1,0:T(8,128)S(1)}, u32[]{:S(2)}, u32[]{:S(2)}) collective-permute-start(f32[5,2,32,512]{3,2,1,0:T(8,128)} %get-tuple-element.10), channel_id=1, source_target_pairs={{4,0},{8,4},{12,8},{16,12},{20,16},{24,20},{28,24},{5,1},{9,5},{13... | collective-permute-start | bytes 1966088 | tf_op jit(solution)/shard_map/ppermute | solution.py:421
  19.5 94.4 %collective-permute-start.2 = (f32[5,2,32,512]{3,2,1,0:T(8,128)}, f32[5,2,32,512]{3,2,1,0:T(8,128)S(1)}, u32[]{:S(2)}, u32[]{:S(2)}) collective-permute-start(f32[5,2,32,512]{3,2,1,0:T(8,128)} %get-tuple-element.11), channel_id=1, source_target_pairs={{0,1},{1,2},{2,3},{4,5},{5,6},{6,7},{8,9},{9,10},{10,11},{12,13},{... | collective-permute-start | bytes 1966088 | tf_op jit(solution)/shard_map/ppermute | solution.py:421
  21.0 92.9 %collective-permute-start.3 = (f32[5,2,32,512]{3,2,1,0:T(8,128)S(1)}, f32[5,2,32,512]{3,2,1,0:T(8,128)S(1)}, u32[]{:S(2)}, u32[]{:S(2)}) collective-permute-start(f32[5,2,32,512]{3,2,1,0:T(8,128)S(1)} %get-tuple-element.12), channel_id=1, source_target_pairs={{1,0},{2,1},{3,2},{5,4},{6,5},{7,6},{9,8},{10,9},{11,10},{13,12},{... | collective-permute-start | bytes 1966088 | tf_op jit(solution)/shard_map/ppermute | solution.py:421
  81.2 1.2 copy-start.5
  82.4 1.2 copy-start.6
  83.7 1.2 copy-start.7
  84.9 1.0 copy-start.8
  85.9 28.0 %copy-start = (f32[4,4,32,128]{3,2,1,0:T(8,128)S(1)}, f32[4,4,32,128]{3,2,1,0:T(8,128)}, u32[]{:S(2)}) copy-start(f32[4,4,32,128]{3,2,1,0:T(8,128)} %constant.103.clone.ay) | copy-start | bytes 786436
  85.9 28.0 %copy-start.3 = (f32[8,64]{1,0:T(8,128)S(1)}, f32[8,64]{1,0:T(8,128)}, u32[]{:S(2)}) copy-start(f32[8,64]{1,0:T(8,128)} %constant.102.clone.ax) | copy-start | bytes 6148

commit v3 on v2

--- a/solution.py
+++ b/solution.py
@@ -13,7 +13,7 @@
 far_coef = 1.0 / 36.0
 time_step = 0.4
 highest = lax.Precision.HIGHEST
-vmem_bytes = 50 * 1024 * 1024
+vmem_bytes = 63 * 1024 * 1024
 
 
 def line_matrices(length):
@@ -25,12 +25,6 @@
     spread[rows, rows + 4] += far_coef
     spread[rows, rows] -= far_coef
     return np.linalg.inv(matrix), spread
-
-
-def split_table(table):
-    table = np.asarray(table, np.float32)
-    high = table.astype(jnp.bfloat16).astype(np.float32)
-    return high, (table - high).astype(jnp.bfloat16).astype(np.float32)
 
 
 def scaled_rows(table, diagonal):
@@ -118,7 +112,7 @@
     return high, (value - high.astype(jnp.float32)).astype(jnp.bfloat16)
 
 
-def edge_kernel(place, cx, cy, weights, rho, mom, ene, xlo, xhi, ylo, yhi, ysum, *, cells, tile, last):
+def edge_kernel(place, cx, cy, weights, _, rho, mom, ene, xlo, xhi, ylo, yhi, ysum, *, cells, tile, last):
     step = pl.program_id(0)
     px, py = place[0], place[1]
     zs = rho.shape[2] // 128
@@ -245,12 +239,17 @@
 
         lax.fori_loop(0, (tile // 2) * 2 * zs, piece, 0)
         half = width // 2
+        slots = hg.shape[2]
+        own_slot = jnp.where(
+            lax.broadcasted_iota(jnp.int32, (rows, slots), 1) % cells
+            == lax.broadcasted_iota(jnp.int32, (rows, slots), 0) // cells + step * tile,
+            1.0, 0.0,
+        )
         for f in range(5):
             base = rho if f == 0 else ene if f == 4 else mom.at[f - 1]
             y_part = dot(my_buf[...], g_buf[f])
-            g_hi, g_lo = split(hg[f])
-            g_hi, g_lo = g_hi.astype(jnp.float32), g_lo.astype(jnp.float32)
-            ghost = jnp.concatenate([g_hi, g_lo, g_hi], axis=0).astype(bf16)
+            g_hi, g_lo = split(jnp.concatenate([hg[f]] * tile, axis=0) * own_slot)
+            ghost = jnp.concatenate([g_hi, g_lo], axis=1)
             for k in range(2):
                 low = 0 if k == 0 else half - 128
                 high = half + 128 if k == 0 else width
@@ -258,10 +257,7 @@
                 weight = mz_buf[low:high, k * half : (k + 1) * half]
                 z_part = dot(left, jnp.concatenate([weight, weight], axis=0))
                 edge = slice(0, 128) if k == 0 else slice(width - 128, width)
-                ends = lax.dot_general(
-                    ghost, wz[:, edge].astype(bf16), (((0,), (0,)), ((), ())),
-                    preferred_element_type=jnp.float32,
-                )
+                ends = dot(ghost, wz[:, edge].astype(bf16))
                 for a, b in chunks[k * zs // 2 : (k + 1) * zs // 2]:
                     got = z_part[:, a - k * half : b - k * half]
                     if a == edge.start:
@@ -280,61 +276,137 @@
                 out[f, :, :, a:b] = acc[f, :, pl.ds(at, 8), a:b] + part
 
 
-def join_kernel(place, ax, ay, acc, xlo, xhi, ylo, yhi, out, *, cells, tile):
+def join_kernel(place, ax, ay, acc, xlo, xhi, ylo, yhi, out, *, cells, tile, last):
     step = pl.program_id(0)
     px = place[0]
     zs = acc.shape[3] // 128
 
     def piece(n, _):
         zc = pl.ds(pl.multiple_of(n * 128, 128), 128)
-        for x in range(tile):
-            i = step * tile + x
-            at_low = jnp.where(i == 0, 0, 1)
-            at_high = jnp.where(i == cells - 1, 0, 1)
-            cl, ch = ax[px, i], ax[px, cells + i]
+        weights = [(ax[px, step * tile + x], ax[px, cells + step * tile + x]) for x in range(tile)]
+        for yy in range(0, cells, 8):
+            ys = slice(yy, yy + 8)
+            a_low, a_high = ay[0, 1, ys], ay[0, 3, ys]
             for f in range(5):
-                y_low, y_high = ylo[f, 1, x : x + 1, zc], yhi[f, 1, x : x + 1, zc]
-                for yy in range(0, cells, 8):
-                    ys = slice(yy, yy + 8)
-                    term = acc[f, x, ys, zc] + cl * xlo[f, at_low, ys, zc] + ch * xhi[f, at_high, ys, zc]
-                    term += ay[0, 1, ys] * y_low + ay[0, 3, ys] * y_high
+                x_low, x_high = xlo[f, 1, ys, zc], xhi[f, 1, ys, zc]
+                for x in range(tile):
+                    row = slice(x, x + 1)
+                    term = acc[f, x, ys, zc] + weights[x][0] * x_low + weights[x][1] * x_high
+                    term += a_low * ylo[f, 1, row, zc] + a_high * yhi[f, 1, row, zc]
                     if yy == 0:
-                        term += ay[0, 0, ys] * ylo[f, 0, x : x + 1, zc]
+                        term += ay[0, 0, ys] * ylo[f, 0, row, zc]
                     if yy + 8 == cells:
-                        term += ay[0, 2, ys] * yhi[f, 0, x : x + 1, zc]
+                        term += ay[0, 2, ys] * yhi[f, 0, row, zc]
                     out[f, x, ys, zc] = term
         return 0
 
     lax.fori_loop(0, zs, piece, 0)
 
-
-def ghost_fluxes(coarse_rows, ghost_rows, time_index, groups_x, place_x, cells):
+    @pl.when(step == 0)
+    def _():
+        for f in range(5):
+            out[f, 0] += xlo[f, 0]
+
+    @pl.when(step == last)
+    def _():
+        for f in range(5):
+            out[f, tile - 1] += xhi[f, 0]
+
+
+def ghost_kernel(rows_ref, time_ref, coarse, out, sent, got, send_sem, recv_sem, *, groups, cells):
+    me = lax.axis_index("gx")
+    slots = rows_ref.shape[1]
+    block = coarse.shape[2]
+    cap = slots // groups
+    f32 = jnp.float32
+    highest_dot = functools.partial(
+        lax.dot_general, precision=highest, preferred_element_type=f32
+    )
+    barrier = pltpu.get_barrier_semaphore()
+    for off in range(1, groups):
+        pl.semaphore_signal(
+            barrier, inc=1, device_id={"gx": lax.rem(me + off, groups)}, device_id_type=pl.DeviceIdType.MESH
+        )
+
+    rows = rows_ref[...]
+    first = me * block
+    mine = jnp.where((rows >= first) & (rows < first + block), 1.0, 0.0)
+    upper = jnp.where(
+        lax.broadcasted_iota(jnp.int32, (slots, slots), 0) <= lax.broadcasted_iota(jnp.int32, (slots, slots), 1),
+        1.0, 0.0,
+    )
+    rank = jnp.where(mine > 0.5, jnp.dot(mine, upper, preferred_element_type=f32) - 1.0, -1.0)
+    wanted = lax.broadcasted_iota(jnp.int32, (cap, slots), 0).astype(f32)
+    local_rows = (rows - first).astype(f32)
+    level = time_ref[...].astype(f32) * 0.125
+    picked, levels = [], []
+    for a in range(groups):
+        pick = rank[a : a + 1] == wanted
+        picked.append(jnp.sum(jnp.where(pick, local_rows[a : a + 1], 0.0), axis=1, keepdims=True))
+        levels.append(jnp.sum(jnp.where(pick, level[a : a + 1], 0.0), axis=1, keepdims=True))
+    picked = jnp.concatenate(picked, axis=0)
+    levels = jnp.concatenate(levels, axis=0)
+    onehot = jnp.where(
+        picked == lax.broadcasted_iota(jnp.int32, (slots, block), 1).astype(f32), 1.0, 0.0
+    )
+    contract = (((1,), (1,)), ((), ()))
+    old = highest_dot(onehot, coarse[0], contract)
+    new = highest_dot(onehot, coarse[1], contract)
+    sent[...] = (1.0 - levels) * old + levels * new
+
+    pl.semaphore_wait(barrier, groups - 1)
+    here = pl.ds(pl.multiple_of(me * cap, cap), cap)
+    copies = []
+    for off in range(1, groups):
+        target = lax.rem(me + off, groups)
+        copy = pltpu.make_async_remote_copy(
+            src_ref=sent.at[pl.ds(pl.multiple_of(target * cap, cap), cap)],
+            dst_ref=got.at[here],
+            send_sem=send_sem.at[off],
+            recv_sem=recv_sem.at[off],
+            device_id={"gx": target},
+            device_id_type=pl.DeviceIdType.MESH,
+        )
+        copy.start()
+        copies.append(copy)
+    got[here] = sent[here]
+    own = rows_ref[pl.ds(me, 1)]
+    source = lax.broadcasted_iota(jnp.int32, (groups, slots), 0) * block
+    match = jnp.where((own >= source) & (own < source + block), 1.0, 0.0)
+    nth = jnp.dot(match, upper, preferred_element_type=f32) - 1.0
+    base = lax.broadcasted_iota(jnp.int32, (groups, slots), 0).astype(f32) * cap
+    index = jnp.sum(match * (nth + base), axis=0, keepdims=True)
+    back = jnp.where(lax.broadcasted_iota(jnp.int32, (slots, slots), 0).astype(f32) == index, 1.0, 0.0)
+    for copy in copies:
+        copy.wait()
+    ghosts = highest_dot(got[...], back, (((0,), (0,)), ((), ())))
+    fields = [ghosts[f * cells : (f + 1) * cells] for f in range(5)]
+    for f, value in enumerate(flux_from(fields, common(fields), 2)):
+        out[f] = value
+
+
+def ghost_fluxes(coarse_rows, ghost_rows, time_index, cells):
+    groups = lax.axis_size("gx")
     slots = ghost_rows.shape[2]
-    capacity = slots // groups_x
-    block = coarse_rows.shape[1]
-    rows = ghost_rows[0]
-    weights = time_index[0].astype(jnp.float32) * 0.125
-    mine = (rows // block == place_x).astype(jnp.int32)
-    upper = (np.arange(slots)[:, None] <= np.arange(slots)[None, :]).astype(np.float32)
-    rank = jnp.dot(mine.astype(jnp.float32), upper, precision=highest).astype(jnp.int32) - 1
-    wanted = jnp.arange(capacity, dtype=jnp.int32)
-    pick = (mine[:, None, :] > 0) & (rank[:, None, :] == wanted[None, :, None])
-    local_rows = jnp.sum(jnp.where(pick, (rows - place_x * block)[:, None, :], 0), axis=2).reshape(-1)
-    level = jnp.sum(jnp.where(pick, weights[:, None, :], 0.0), axis=2).reshape(-1, 1)
-    onehot = (local_rows[:, None] == jnp.arange(block)[None, :]).astype(jnp.float32)
-    old = jnp.dot(onehot, coarse_rows[0, :, 0, :], precision=highest)
-    new = jnp.dot(onehot, coarse_rows[1, :, 0, :], precision=highest)
-    sent = ((1.0 - level) * old + level * new).reshape(groups_x, capacity, -1)
-    every = lax.all_gather(sent, "gx")
-    got = lax.dynamic_index_in_dim(every, place_x, 1, keepdims=False).reshape(slots, -1)
-    owner = lax.dynamic_index_in_dim(rows, place_x, 0, keepdims=False) // block
-    earlier = np.arange(slots)[None, :] < np.arange(slots)[:, None]
-    nth = jnp.sum(((owner[:, None] == owner[None, :]) & earlier).astype(jnp.int32), axis=1)
-    back = ((owner * capacity + nth)[:, None] == jnp.arange(slots)[None, :]).astype(jnp.float32)
-    ghosts = jnp.dot(back, got, precision=highest).reshape(4, cells, 5, cells)
-    fields = [ghosts[:, :, f] for f in range(5)]
-    flux = jnp.stack(flux_from(fields, common(fields), 2)).reshape(5, 4, cells * cells)
-    return jnp.pad(flux, ((0, 0), (0, 4), (0, 0)))
+    width = coarse_rows.shape[3]
+    vmem = pl.BlockSpec(memory_space=pltpu.VMEM)
+    return pl.pallas_call(
+        functools.partial(ghost_kernel, groups=groups, cells=cells),
+        out_shape=jax.ShapeDtypeStruct((5, cells, slots), jnp.float32),
+        in_specs=[vmem] * 3,
+        out_specs=vmem,
+        scratch_shapes=[
+            pltpu.VMEM((slots, width), jnp.float32),
+            pltpu.VMEM((slots, width), jnp.float32),
+            pltpu.SemaphoreType.DMA((groups,)),
+            pltpu.SemaphoreType.DMA((groups,)),
+        ],
+        compiler_params=pltpu.CompilerParams(
+            collective_id=0, has_side_effects=True, vmem_limit_bytes=vmem_bytes
+        ),
+        cost_estimate=pl.CostEstimate(flops=1 << 24, bytes_accessed=1 << 20, transcendentals=0),
+        name="ghosts",
+    )(ghost_rows[0], time_index[0], coarse_rows[:, :, 0, :].transpose(0, 2, 1))
 
 
 def local(density, momentum, energy, coarse_rows, ghost_rows, time_index):
@@ -354,25 +426,22 @@
     at_y = np.tile(np.arange(cells), groups_y)
     scale_x, values_x = scaled_rows(own_x.reshape(-1, cells), at_x)
     scale_y, values_y = scaled_rows(own_y.reshape(-1, cells), at_y)
-    scale_z, values_z = scaled_rows(whole_z[:, 2:-2], np.arange(cells_z))
+    scale_z, values_z = scaled_rows(whole_z, np.arange(cells_z) + 2)
     lanes = np.ones((1, 128), np.float32)
     mx = np.stack([np.kron(m, np.eye(8)) for m in values_x.reshape(own_x.shape)]).astype(np.float32)
     my = np.stack([np.kron(np.eye(tile), m) for m in values_y.reshape(own_y.shape)]).astype(np.float32)
-    mz = np.ascontiguousarray(values_z.T)
+    mz = np.ascontiguousarray(values_z[:, 2:-2].T)
     sx = np.stack([np.repeat(v, 8)[:, None] * lanes for v in scale_x.reshape(groups_x, cells)])
     sy = np.stack([np.tile(v, tile)[:, None] * lanes for v in scale_y.reshape(groups_y, cells)])
     sx, sy, sz = sx.astype(np.float32), sy.astype(np.float32), scale_z[None, :].astype(np.float32)
-    ends = np.zeros((8, cells_z), np.float32)
-    ends[:4] = (whole_z[:, [0, 1, cells_z + 2, cells_z + 3]] / scale_z[:, None]).T
-    ends_hi, ends_lo = split_table(ends)
-    wz = np.concatenate([ends_hi, ends_hi, ends_lo])
+    wz = np.tile(np.repeat(values_z[:, [0, 1, cells_z + 2, cells_z + 3]].T, cells, axis=0), (2, 1))
     cy = edge_scalars(beyond_y, cells).astype(np.float32)
     weights = np.broadcast_to(beyond_y[:, 1::2, :, None], (groups_y, 2, cells, 128)).astype(np.float32)
     cx = edge_scalars(beyond_x, cells).astype(np.float32)
-    ax = np.concatenate([act_x[:, 0] + act_x[:, 1], act_x[:, 2] + act_x[:, 3]], axis=1).astype(np.float32)
+    ax = np.concatenate([act_x[:, 1], act_x[:, 3]], axis=1).astype(np.float32)
     ay = np.broadcast_to(act_y[..., None], act_y.shape + (128,)).astype(np.float32)
 
-    hg = ghost_fluxes(coarse_rows, ghost_rows, time_index, groups_x, place_x, cells)
+    hg = ghost_fluxes(coarse_rows, ghost_rows, time_index, cells)
 
     smem = pl.BlockSpec(memory_space=pltpu.SMEM)
     xtile3 = pl.BlockSpec((tile, cells, cells_z), lambda i, p: (i, 0, 0))
@@ -408,13 +477,13 @@
     bf16 = jnp.bfloat16
     xlo, xhi, ylo, yhi = call(
         functools.partial(edge_kernel, cells=cells, tile=tile, last=steps - 1),
-        [smem, smem, fixed(weights, 1), xtile3, xtile4, xtile3],
+        [smem, smem, fixed(weights, 1), pl.BlockSpec(memory_space=pl.ANY), xtile3, xtile4, xtile3],
         [planes] * 4,
         [xplane, xplane, yplane, yplane],
         [pltpu.VMEM((5, 2, tile, 8, 128), f32)],
         (size * 20, size),
         name="edges",
-    )(place, cx, cy, weights, density, momentum, energy)
+    )(place, cx, cy, weights, hg, density, momentum, energy)
 
     def shift(array, axis, by):
         peers = lax.axis_size(axis)
@@ -432,7 +501,7 @@
         functools.partial(lines_kernel, cells=cells, tile=tile, steps=steps),
         [
             fixed(mx, 0), fixed(my, 1), fixed(mz), fixed(wz), fixed(sx, 0), fixed(sy, 1), fixed(sz),
-            pl.BlockSpec((5, 8, rows), lambda i, p: (0, 0, jnp.minimum(i, top))),
+            fixed(hg),
             pl.BlockSpec((tile, cells, cells_z), lambda i, p: (jnp.minimum(i, top), 0, 0)),
             pl.BlockSpec((3, tile, cells, cells_z), lambda i, p: (0, jnp.minimum(i, top), 0, 0)),
             pl.BlockSpec((tile, cells, cells_z), lambda i, p: (jnp.minimum(i, top), 0, 0)),
@@ -453,7 +522,7 @@
         name="lines",
     )(place, mx, my, mz, wz, sx, sy, sz, hg, density, momentum, energy)
     return call(
-        functools.partial(join_kernel, cells=cells, tile=tile),
+        functools.partial(join_kernel, cells=cells, tile=tile, last=steps - 1),
         [smem, fixed(ay, 1), xtile5, xplane, xplane, yplane, yplane],
         whole,
         xtile5,

time: 126 us -> 74.6 us (0.59)
  the two profiles are of different devices: /device:TPU:0 before, /device:TPU:29 now
where the time goes in v3:
time: 74.6 us; the launch traced here: 74.4 us
  Pallas kernels  59.4 us (80%)
  starting transfers between devices  13.5 us (18%)
  local copies, waits for them, and re-layouts  0.82 us (1%)
    pallas_call x1, Pallas kernels, local(): call(functools.partial(lines_kernel, cells=cells, tile=tile, steps=steps)...  29.1 us
    ppermute x4, starting transfers between devices, shift(): lax.ppermute(array, axis, [(i, i + by) for i in range(peers) if 0 <= i +...  13.5 us
    pallas_call x1, Pallas kernels, local(): call(functools.partial(edge_kernel, cells=cells, tile=tile, last=steps -...  11.1 us
    pallas_call x1, Pallas kernels, local(): call(functools.partial(join_kernel, cells=cells, tile=tile, last=steps -...  10.8 us
    pallas_call x1, Pallas kernels, ghost_fluxes(): pl.pallas_call(functools.partial(ghost_kernel, groups=groups, cells=cells...  8.36 us
  transfers between devices with their start and end apart: 4, of which 0 were waited for; matrix products, arithmetic and copies ran while one was open for 0% of the time, Pallas kernels for 39%

profile of v3, /device:TPU:29, one launch (start us, length us, event | category | flops | bytes accessed | tf_op | source)
XLA Modules:
  0.0 74.4 jit_solution(13518497380537435465)
XLA Ops:
  0.0 0.6 pad_add_fusion.place
  0.6 8.4 %ghosts.1.hg._ = f32[5,32,128]{2,1,0:T(8,128)} custom-call(s32[8,128]{1,0:T(8,128)} %bitcast.8, s32[8,128]{1,0:T(8,128)} %bitcast.9, f32[2,160,256]{2,1,0:T(8,128)} %bitcast.7), custom_call_target="tpu_custom_call" | custom-call | flops 16777216 | bytes 1048576 | tf_op jit(solution)/shard_map/ghosts/pallas_call | solution.py:393
  9.0 11.1 %edges.1 = (f32[5,2,32,512]{3,2,1,0:T(8,128)}, f32[5,2,32,512]{3,2,1,0:T(8,128)}, f32[5,2,32,512]{3,2,1,0:T(8,128)}, f32[5,2,32,512]{3,2,1,0:T(8,128)}) custom-call(s32[2]{0:T(128)} %pad_add_fusion.place, f32[8,68]{1,0:T(8,128)} %constant.33.clone.cx, f32[4,68]{1,0:T(4,128)} %constant.34.clone.cy, f32[4,2,32,128]{3,2,1,0:T(8,128)} %constant.35.clone.weights, ...), custom_call_target="tpu_custom_call" | custom-call | flops 209715200 | bytes 10485760 | tf_op jit(solution)/shard_map/edges/pallas_call | solution.py:478
  20.0 1.3 %collective-permute-start = (f32[5,2,32,512]{3,2,1,0:T(8,128)}, f32[5,2,32,512]{3,2,1,0:T(8,128)S(1)}, u32[]{:S(2)}, u32[]{:S(2)}) collective-permute-start(f32[5,2,32,512]{3,2,1,0:T(8,128)} %get-tuple-element.9), channel_id=1, source_target_pairs={{0,4},{4,8},{8,12},{12,16},{16,20},{20,24},{24,28},{1,5},{5,9},{9,... | collective-permute-start | bytes 1966088 | tf_op jit(solution)/shard_map/ppermute | solution.py:490
  21.3 4.8 %collective-permute-start.1 = (f32[5,2,32,512]{3,2,1,0:T(8,128)}, f32[5,2,32,512]{3,2,1,0:T(8,128)}, u32[]{:S(2)}, u32[]{:S(2)}) collective-permute-start(f32[5,2,32,512]{3,2,1,0:T(8,128)} %get-tuple-element.10), channel_id=1, source_target_pairs={{4,0},{8,4},{12,8},{16,12},{20,16},{24,20},{28,24},{5,1},{9,5},{13... | collective-permute-start | bytes 1966088 | tf_op jit(solution)/shard_map/ppermute | solution.py:490
  26.2 5.4 %collective-permute-start.2 = (f32[5,2,32,512]{3,2,1,0:T(8,128)}, f32[5,2,32,512]{3,2,1,0:T(8,128)}, u32[]{:S(2)}, u32[]{:S(2)}) collective-permute-start(f32[5,2,32,512]{3,2,1,0:T(8,128)} %get-tuple-element.11), channel_id=1, source_target_pairs={{0,1},{1,2},{2,3},{4,5},{5,6},{6,7},{8,9},{9,10},{10,11},{12,13},{... | collective-permute-start | bytes 1966088 | tf_op jit(solution)/shard_map/ppermute | solution.py:490
  31.6 1.9 %collective-permute-start.3 = (f32[5,2,32,512]{3,2,1,0:T(8,128)}, f32[5,2,32,512]{3,2,1,0:T(8,128)}, u32[]{:S(2)}, u32[]{:S(2)}) collective-permute-start(f32[5,2,32,512]{3,2,1,0:T(8,128)} %get-tuple-element.12), channel_id=1, source_target_pairs={{1,0},{2,1},{3,2},{5,4},{6,5},{7,6},{9,8},{10,9},{11,10},{13,12},{... | collective-permute-start | bytes 1966088 | tf_op jit(solution)/shard_map/ppermute | solution.py:490
  33.6 29.1 %lines.1.acc = f32[5,32,32,512]{3,2,1,0:T(8,128)} custom-call(s32[2]{0:T(128)} %pad_add_fusion.place, f32[8,256,256]{2,1,0:T(8,128)} %constant.36.clone.mx, f32[4,256,256]{2,1,0:T(8,128)} %constant.37.clone.my, f32[512,512]{1,0:T(8,128)} %constant.38.clone.mz, f32[256,512]{1,0:T(8,128)} %constant.39.clone.wz, f32[8,256,128]{2,1,0:T(8,128)} %constant.40.clone.sx, ...), custom_call_target="tpu_custom_call" | custom-call | flops 12582912000 | bytes 20971520 | tf_op jit(solution)/shard_map/lines/pallas_call | solution.py:500
  62.7 0.0 collective-permute-done.xlo
  62.7 0.0 copy-start
  62.7 0.0 collective-permute-done.1.xhi
  62.7 0.0 collective-permute-done.2.ylo
  62.7 0.0 collective-permute-done.3.yhi
  62.7 0.8 %copy-done = f32[5,2,32,512]{3,2,1,0:T(8,128)} copy-done((f32[5,2,32,512]{3,2,1,0:T(8,128)}, f32[5,2,32,512]{3,2,1,0:T(8,128)S(1)}, u32[]{:S(2)}) %copy-start) | copy-done | bytes 655384
  63.5 10.8 %join.1 = f32[5,32,32,512]{3,2,1,0:T(8,128)} custom-call(s32[2]{0:T(128)} %pad_add_fusion.place, f32[8,64]{1,0:T(8,128)} %constant.43.clone.ax, f32[4,4,32,128]{3,2,1,0:T(8,128)} %constant.44.clone.ay, f32[5,32,32,512]{3,2,1,0:T(8,128)} %lines.1.acc, f32[5,2,32,512]{3,2,1,0:T(8,128)} %copy-done, f32[5,2,32,512]{3,2,1,0:T(8,128)} %collective-permute-done.1.xhi, ...), custom_call_target="tpu_custom_call" | custom-call | flops 41943040 | bytes 20971520 | tf_op jit(solution)/shard_map/join/pallas_call | solution.py:524
Async XLA Ops:
  20.0 42.6 %collective-permute-start = (f32[5,2,32,512]{3,2,1,0:T(8,128)}, f32[5,2,32,512]{3,2,1,0:T(8,128)S(1)}, u32[]{:S(2)}, u32[]{:S(2)}) collective-permute-start(f32[5,2,32,512]{3,2,1,0:T(8,128)} %get-tuple-element.9), channel_id=1, source_target_pairs={{0,4},{4,8},{8,12},{12,16},{16,20},{20,24},{24,28},{1,5},{5,9},{9,... | collective-permute-start | bytes 1966088 | tf_op jit(solution)/shard_map/ppermute | solution.py:490
  21.3 41.4 %collective-permute-start.1 = (f32[5,2,32,512]{3,2,1,0:T(8,128)}, f32[5,2,32,512]{3,2,1,0:T(8,128)}, u32[]{:S(2)}, u32[]{:S(2)}) collective-permute-start(f32[5,2,32,512]{3,2,1,0:T(8,128)} %get-tuple-element.10), channel_id=1, source_target_pairs={{4,0},{8,4},{12,8},{16,12},{20,16},{24,20},{28,24},{5,1},{9,5},{13... | collective-permute-start | bytes 1966088 | tf_op jit(solution)/shard_map/ppermute | solution.py:490
  26.2 36.5 %collective-permute-start.2 = (f32[5,2,32,512]{3,2,1,0:T(8,128)}, f32[5,2,32,512]{3,2,1,0:T(8,128)}, u32[]{:S(2)}, u32[]{:S(2)}) collective-permute-start(f32[5,2,32,512]{3,2,1,0:T(8,128)} %get-tuple-element.11), channel_id=1, source_target_pairs={{0,1},{1,2},{2,3},{4,5},{5,6},{6,7},{8,9},{9,10},{10,11},{12,13},{... | collective-permute-start | bytes 1966088 | tf_op jit(solution)/shard_map/ppermute | solution.py:490
  31.6 31.1 %collective-permute-start.3 = (f32[5,2,32,512]{3,2,1,0:T(8,128)}, f32[5,2,32,512]{3,2,1,0:T(8,128)}, u32[]{:S(2)}, u32[]{:S(2)}) collective-permute-start(f32[5,2,32,512]{3,2,1,0:T(8,128)} %get-tuple-element.12), channel_id=1, source_target_pairs={{1,0},{2,1},{3,2},{5,4},{6,5},{7,6},{9,8},{10,9},{11,10},{13,12},{... | collective-permute-start | bytes 1966088 | tf_op jit(solution)/shard_map/ppermute | solution.py:490
  62.7 0.9 %copy-start = (f32[5,2,32,512]{3,2,1,0:T(8,128)}, f32[5,2,32,512]{3,2,1,0:T(8,128)S(1)}, u32[]{:S(2)}) copy-start(f32[5,2,32,512]{3,2,1,0:T(8,128)S(1)} %collective-permute-done.xlo) | copy-start | bytes 1966084

commit v4 on v2

--- a/solution.py
+++ b/solution.py
@@ -13,7 +13,7 @@
 far_coef = 1.0 / 36.0
 time_step = 0.4
 highest = lax.Precision.HIGHEST
-vmem_bytes = 50 * 1024 * 1024
+vmem_bytes = 63 * 1024 * 1024
 
 
 def line_matrices(length):
@@ -25,12 +25,6 @@
     spread[rows, rows + 4] += far_coef
     spread[rows, rows] -= far_coef
     return np.linalg.inv(matrix), spread
-
-
-def split_table(table):
-    table = np.asarray(table, np.float32)
-    high = table.astype(jnp.bfloat16).astype(np.float32)
-    return high, (table - high).astype(jnp.bfloat16).astype(np.float32)
 
 
 def scaled_rows(table, diagonal):
@@ -118,13 +112,110 @@
     return high, (value - high.astype(jnp.float32)).astype(jnp.bfloat16)
 
 
-def edge_kernel(place, cx, cy, weights, rho, mom, ene, xlo, xhi, ylo, yhi, ysum, *, cells, tile, last):
+def ghost_copies(sent, got, send_sem, recv_sem, groups):
+    me = lax.axis_index("gx")
+    cap = sent.shape[0] // groups
+    copies = []
+    for off in range(1, groups):
+        target = lax.rem(me + off, groups)
+        copies.append(
+            pltpu.make_async_remote_copy(
+                src_ref=sent.at[pl.ds(pl.multiple_of(target * cap, cap), cap)],
+                dst_ref=got.at[pl.ds(pl.multiple_of(me * cap, cap), cap)],
+                send_sem=send_sem.at[off],
+                recv_sem=recv_sem.at[off],
+                device_id={"gx": target},
+                device_id_type=pl.DeviceIdType.MESH,
+            )
+        )
+    return copies
+
+
+def up_to(slots):
+    row = lax.broadcasted_iota(jnp.int32, (slots, slots), 0)
+    return jnp.where(row <= lax.broadcasted_iota(jnp.int32, (slots, slots), 1), 1.0, 0.0)
+
+
+def send_ghosts(rows_ref, time_ref, coarse, sent, got, send_sem, recv_sem, groups):
+    me = lax.axis_index("gx")
+    slots = rows_ref.shape[1]
+    block = coarse.shape[2]
+    cap = slots // groups
+    f32 = jnp.float32
+    highest_dot = functools.partial(
+        lax.dot_general, precision=highest, preferred_element_type=f32
+    )
+    barrier = pltpu.get_barrier_semaphore()
+    for off in range(1, groups):
+        pl.semaphore_signal(
+            barrier, inc=1, device_id={"gx": lax.rem(me + off, groups)}, device_id_type=pl.DeviceIdType.MESH
+        )
+
+    rows = rows_ref[...]
+    first = me * block
+    mine = jnp.where((rows >= first) & (rows < first + block), 1.0, 0.0)
+    upper = up_to(slots)
+    rank = jnp.where(mine > 0.5, jnp.dot(mine, upper, preferred_element_type=f32) - 1.0, -1.0)
+    wanted = lax.broadcasted_iota(jnp.int32, (cap, slots), 0).astype(f32)
+    local_rows = (rows - first).astype(f32)
+    level = time_ref[...].astype(f32) * 0.125
+    picked, levels = [], []
+    for a in range(groups):
+        pick = rank[a : a + 1] == wanted
+        picked.append(jnp.sum(jnp.where(pick, local_rows[a : a + 1], 0.0), axis=1, keepdims=True))
+        levels.append(jnp.sum(jnp.where(pick, level[a : a + 1], 0.0), axis=1, keepdims=True))
+    picked = jnp.concatenate(picked, axis=0)
+    levels = jnp.concatenate(levels, axis=0)
+    onehot = jnp.where(
+        picked == lax.broadcasted_iota(jnp.int32, (slots, block), 1).astype(f32), 1.0, 0.0
+    )
+    contract = (((1,), (1,)), ((), ()))
+    old = highest_dot(onehot, coarse[0], contract)
+    new = highest_dot(onehot, coarse[1], contract)
+    sent[...] = (1.0 - levels) * old + levels * new
+
+    pl.semaphore_wait(barrier, groups - 1)
+    for copy in ghost_copies(sent, got, send_sem, recv_sem, groups):
+        copy.start()
+    here = pl.ds(pl.multiple_of(me * cap, cap), cap)
+    got[here] = sent[here]
+
+
+def finish_ghosts(rows_ref, block, out, sent, got, send_sem, recv_sem, groups, cells):
+    me = lax.axis_index("gx")
+    slots = rows_ref.shape[1]
+    cap = slots // groups
+    f32 = jnp.float32
+    highest_dot = functools.partial(
+        lax.dot_general, precision=highest, preferred_element_type=f32
+    )
+    upper = up_to(slots)
+    own = rows_ref[pl.ds(me, 1)]
+    source = lax.broadcasted_iota(jnp.int32, (groups, slots), 0) * block
+    match = jnp.where((own >= source) & (own < source + block), 1.0, 0.0)
+    nth = jnp.dot(match, upper, preferred_element_type=f32) - 1.0
+    base = lax.broadcasted_iota(jnp.int32, (groups, slots), 0).astype(f32) * cap
+    index = jnp.sum(match * (nth + base), axis=0, keepdims=True)
+    back = jnp.where(lax.broadcasted_iota(jnp.int32, (slots, slots), 0).astype(f32) == index, 1.0, 0.0)
+    for copy in ghost_copies(sent, got, send_sem, recv_sem, groups):
+        copy.wait()
+    ghosts = highest_dot(got[...], back, (((0,), (0,)), ((), ())))
+    fields = [ghosts[f * cells : (f + 1) * cells] for f in range(5)]
+    for f, value in enumerate(flux_from(fields, common(fields), 2)):
+        out[f] = value
+
+
+def edge_kernel(
+    cx, cy, weights, rows, times, coarse, rho, mom, ene, xlo, xhi, ylo, yhi, hg,
+    ysum, sent, got, send_sem, recv_sem, *, cells, tile, last, groups
+):
     step = pl.program_id(0)
-    px, py = place[0], place[1]
+    px, py = lax.axis_index("gx"), lax.axis_index("gy")
     zs = rho.shape[2] // 128
 
     @pl.when(step == 0)
     def _():
+        send_ghosts(rows, times, coarse, sent, got, send_sem, recv_sem, groups)
         xlo[...] = jnp.zeros_like(xlo)
         xhi[...] = jnp.zeros_like(xhi)
 
@@ -163,7 +254,7 @@
                 row = pl.ds(x, 1)
                 for f in range(5):
                     for d, out in ((0, ylo), (1, yhi)):
-                        part = side[f] * weights[0, d, ys]
+                        part = side[f] * weights[py, d, ys]
                         part = part[:8] + part[8:]
                         if yy > 0:
                             part += ysum[f, d, x]
@@ -194,9 +285,14 @@
 
     lax.fori_loop(0, zs, piece, 0)
 
+    @pl.when(step == last)
+    def _():
+        finish_ghosts(rows, coarse.shape[2], hg, sent, got, send_sem, recv_sem, groups, cells)
+
 
 def lines_kernel(
-    place, mx, my, mz, wz, sx, sy, sz, hg, rho, mom, ene, out,
+    mx, my, mz, wz, sx, sy, sz, hg, to_low_x, to_high_x, to_low_y, to_high_y, rho, mom, ene,
+    out, low_x, high_x, low_y, high_y, send_sem, recv_sem, keep_sem,
     f_buf, g_buf, h_buf, acc, mx_buf, my_buf, mz_buf, *, cells, tile, steps
 ):
     step = pl.program_id(0)
@@ -207,9 +303,40 @@
     dot = functools.partial(jnp.dot, preferred_element_type=jnp.float32)
     chunks = [(z * 128, (z + 1) * 128) for z in range(zs)]
 
+    moves = []
+    for n, (axis, by, source, target) in enumerate(
+        (("gx", 1, to_high_x, low_x), ("gx", -1, to_low_x, high_x),
+         ("gy", 1, to_high_y, low_y), ("gy", -1, to_low_y, high_y))
+    ):
+        here, count = lax.axis_index(axis), lax.axis_size(axis)
+        sends = here < count - 1 if by > 0 else here > 0
+        gets = here > 0 if by > 0 else here < count - 1
+        copy = pltpu.make_async_remote_copy(
+            src_ref=source, dst_ref=target, send_sem=send_sem.at[n], recv_sem=recv_sem.at[n],
+            device_id={axis: jnp.clip(here + by, 0, count - 1)}, device_id_type=pl.DeviceIdType.MESH,
+        )
+        own = pltpu.make_async_copy(source, target, keep_sem.at[n])
+        moves.append((axis, here + by, sends, gets, copy, own))
+
     @pl.when(step == 0)
     def _():
-        for buf, table in ((mx_buf, mx[0]), (my_buf, my[0])):
+        barrier = pltpu.get_barrier_semaphore()
+        for axis, to, sends, _, _, _ in moves:
+            @pl.when(sends)
+            def _():
+                pl.semaphore_signal(
+                    barrier, inc=1, device_id={axis: to}, device_id_type=pl.DeviceIdType.MESH
+                )
+        pl.semaphore_wait(barrier, sum(jnp.where(gets, 1, 0) for _, _, _, gets, _, _ in moves))
+        for _, _, sends, gets, copy, own in moves:
+            @pl.when(sends)
+            def _():
+                copy.start()
+
+            @pl.when(jnp.logical_not(gets))
+            def _():
+                own.start()
+        for buf, table in ((mx_buf, mx[lax.axis_index("gx")]), (my_buf, my[lax.axis_index("gy")])):
             buf[:, :rows] = table.astype(bf16)
             buf[:, rows:] = table.astype(bf16)
         mz_buf[...] = mz[...].astype(bf16)
@@ -245,12 +372,17 @@
 
         lax.fori_loop(0, (tile // 2) * 2 * zs, piece, 0)
         half = width // 2
+        slots = hg.shape[2]
+        own_slot = jnp.where(
+            lax.broadcasted_iota(jnp.int32, (rows, slots), 1) % cells
+            == lax.broadcasted_iota(jnp.int32, (rows, slots), 0) // cells + step * tile,
+            1.0, 0.0,
+        )
         for f in range(5):
             base = rho if f == 0 else ene if f == 4 else mom.at[f - 1]
             y_part = dot(my_buf[...], g_buf[f])
-            g_hi, g_lo = split(hg[f])
-            g_hi, g_lo = g_hi.astype(jnp.float32), g_lo.astype(jnp.float32)
-            ghost = jnp.concatenate([g_hi, g_lo, g_hi], axis=0).astype(bf16)
+            g_hi, g_lo = split(jnp.concatenate([hg[f]] * tile, axis=0) * own_slot)
+            ghost = jnp.concatenate([g_hi, g_lo], axis=1)
             for k in range(2):
                 low = 0 if k == 0 else half - 128
                 high = half + 128 if k == 0 else width
@@ -258,15 +390,12 @@
                 weight = mz_buf[low:high, k * half : (k + 1) * half]
                 z_part = dot(left, jnp.concatenate([weight, weight], axis=0))
                 edge = slice(0, 128) if k == 0 else slice(width - 128, width)
-                ends = lax.dot_general(
-                    ghost, wz[:, edge].astype(bf16), (((0,), (0,)), ((), ())),
-                    preferred_element_type=jnp.float32,
-                )
+                ends = dot(ghost, wz[:, edge].astype(bf16))
                 for a, b in chunks[k * zs // 2 : (k + 1) * zs // 2]:
                     got = z_part[:, a - k * half : b - k * half]
                     if a == edge.start:
                         got = got + ends
-                    got = got * sz[:, a:b] + y_part[:, a:b] * sy[0]
+                    got = got * sz[:, a:b] + y_part[:, a:b] * sy[lax.axis_index("gy")]
                     acc[f, pl.ds(step * tile, tile), :, a:b] = base[:, :, a:b] + got.reshape(tile, cells, 128)
 
     @pl.when(step >= steps)
@@ -276,65 +405,60 @@
         for f in range(5):
             got = dot(mx_buf[...], f_buf[j, f])
             for a, b in chunks:
-                part = (got[:, a:b] * sx[0]).reshape(cells, 8, 128)
+                part = (got[:, a:b] * sx[lax.axis_index("gx")]).reshape(cells, 8, 128)
                 out[f, :, :, a:b] = acc[f, :, pl.ds(at, 8), a:b] + part
 
-
-def join_kernel(place, ax, ay, acc, xlo, xhi, ylo, yhi, out, *, cells, tile):
+    @pl.when(step == 2 * steps - 1)
+    def _():
+        for _, _, sends, gets, copy, own in moves:
+            @pl.when(sends)
+            def _():
+                copy.wait_send()
+
+            @pl.when(gets)
+            def _():
+                copy.wait_recv()
+
+            @pl.when(jnp.logical_not(gets))
+            def _():
+                own.wait()
+
+
+def join_kernel(place, ax, ay, acc, xlo, xhi, ylo, yhi, out, *, cells, tile, last, groups):
     step = pl.program_id(0)
     px = place[0]
     zs = acc.shape[3] // 128
 
     def piece(n, _):
         zc = pl.ds(pl.multiple_of(n * 128, 128), 128)
-        for x in range(tile):
-            i = step * tile + x
-            at_low = jnp.where(i == 0, 0, 1)
-            at_high = jnp.where(i == cells - 1, 0, 1)
-            cl, ch = ax[px, i], ax[px, cells + i]
+        weights = [(ax[px, step * tile + x], ax[px, cells + step * tile + x]) for x in range(tile)]
+        for yy in range(0, cells, 8):
+            ys = slice(yy, yy + 8)
+            a_low, a_high = ay[0, 1, ys], ay[0, 3, ys]
             for f in range(5):
-                y_low, y_high = ylo[f, 1, x : x + 1, zc], yhi[f, 1, x : x + 1, zc]
-                for yy in range(0, cells, 8):
-                    ys = slice(yy, yy + 8)
-                    term = acc[f, x, ys, zc] + cl * xlo[f, at_low, ys, zc] + ch * xhi[f, at_high, ys, zc]
-                    term += ay[0, 1, ys] * y_low + ay[0, 3, ys] * y_high
+                x_low, x_high = xlo[f, 1, ys, zc], xhi[f, 1, ys, zc]
+                for x in range(tile):
+                    row = slice(x, x + 1)
+                    term = acc[f, x, ys, zc] + weights[x][0] * x_low + weights[x][1] * x_high
+                    term += a_low * ylo[f, 1, row, zc] + a_high * yhi[f, 1, row, zc]
                     if yy == 0:
-                        term += ay[0, 0, ys] * ylo[f, 0, x : x + 1, zc]
+                        term += ay[0, 0, ys] * ylo[f, 0, row, zc]
                     if yy + 8 == cells:
-                        term += ay[0, 2, ys] * yhi[f, 0, x : x + 1, zc]
+                        term += ay[0, 2, ys] * yhi[f, 0, row, zc]
                     out[f, x, ys, zc] = term
         return 0
 
     lax.fori_loop(0, zs, piece, 0)
 
-
-def ghost_fluxes(coarse_rows, ghost_rows, time_index, groups_x, place_x, cells):
-    slots = ghost_rows.shape[2]
-    capacity = slots // groups_x
-    block = coarse_rows.shape[1]
-    rows = ghost_rows[0]
-    weights = time_index[0].astype(jnp.float32) * 0.125
-    mine = (rows // block == place_x).astype(jnp.int32)
-    upper = (np.arange(slots)[:, None] <= np.arange(slots)[None, :]).astype(np.float32)
-    rank = jnp.dot(mine.astype(jnp.float32), upper, precision=highest).astype(jnp.int32) - 1
-    wanted = jnp.arange(capacity, dtype=jnp.int32)
-    pick = (mine[:, None, :] > 0) & (rank[:, None, :] == wanted[None, :, None])
-    local_rows = jnp.sum(jnp.where(pick, (rows - place_x * block)[:, None, :], 0), axis=2).reshape(-1)
-    level = jnp.sum(jnp.where(pick, weights[:, None, :], 0.0), axis=2).reshape(-1, 1)
-    onehot = (local_rows[:, None] == jnp.arange(block)[None, :]).astype(jnp.float32)
-    old = jnp.dot(onehot, coarse_rows[0, :, 0, :], precision=highest)
-    new = jnp.dot(onehot, coarse_rows[1, :, 0, :], precision=highest)
-    sent = ((1.0 - level) * old + level * new).reshape(groups_x, capacity, -1)
-    every = lax.all_gather(sent, "gx")
-    got = lax.dynamic_index_in_dim(every, place_x, 1, keepdims=False).reshape(slots, -1)
-    owner = lax.dynamic_index_in_dim(rows, place_x, 0, keepdims=False) // block
-    earlier = np.arange(slots)[None, :] < np.arange(slots)[:, None]
-    nth = jnp.sum(((owner[:, None] == owner[None, :]) & earlier).astype(jnp.int32), axis=1)
-    back = ((owner * capacity + nth)[:, None] == jnp.arange(slots)[None, :]).astype(jnp.float32)
-    ghosts = jnp.dot(back, got, precision=highest).reshape(4, cells, 5, cells)
-    fields = [ghosts[:, :, f] for f in range(5)]
-    flux = jnp.stack(flux_from(fields, common(fields), 2)).reshape(5, 4, cells * cells)
-    return jnp.pad(flux, ((0, 0), (0, 4), (0, 0)))
+    @pl.when((step == 0) & (px > 0))
+    def _():
+        for f in range(5):
+            out[f, 0] += xlo[f, 0]
+
+    @pl.when((step == last) & (px < groups - 1))
+    def _():
+        for f in range(5):
+            out[f, tile - 1] += xhi[f, 0]
 
 
 def local(density, momentum, energy, coarse_rows, ghost_rows, time_index):
@@ -354,92 +478,97 @@
     at_y = np.tile(np.arange(cells), groups_y)
     scale_x, values_x = scaled_rows(own_x.reshape(-1, cells), at_x)
     scale_y, values_y = scaled_rows(own_y.reshape(-1, cells), at_y)
-    scale_z, values_z = scaled_rows(whole_z[:, 2:-2], np.arange(cells_z))
+    scale_z, values_z = scaled_rows(whole_z, np.arange(cells_z) + 2)
     lanes = np.ones((1, 128), np.float32)
     mx = np.stack([np.kron(m, np.eye(8)) for m in values_x.reshape(own_x.shape)]).astype(np.float32)
     my = np.stack([np.kron(np.eye(tile), m) for m in values_y.reshape(own_y.shape)]).astype(np.float32)
-    mz = np.ascontiguousarray(values_z.T)
+    mz = np.ascontiguousarray(values_z[:, 2:-2].T)
     sx = np.stack([np.repeat(v, 8)[:, None] * lanes for v in scale_x.reshape(groups_x, cells)])
     sy = np.stack([np.tile(v, tile)[:, None] * lanes for v in scale_y.reshape(groups_y, cells)])
     sx, sy, sz = sx.astype(np.float32), sy.astype(np.float32), scale_z[None, :].astype(np.float32)
-    ends = np.zeros((8, cells_z), np.float32)
-    ends[:4] = (whole_z[:, [0, 1, cells_z + 2, cells_z + 3]] / scale_z[:, None]).T
-    ends_hi, ends_lo = split_table(ends)
-    wz = np.concatenate([ends_hi, ends_hi, ends_lo])
+    wz = np.tile(np.repeat(values_z[:, [0, 1, cells_z + 2, cells_z + 3]].T, cells, axis=0), (2, 1))
     cy = edge_scalars(beyond_y, cells).astype(np.float32)
     weights = np.broadcast_to(beyond_y[:, 1::2, :, None], (groups_y, 2, cells, 128)).astype(np.float32)
     cx = edge_scalars(beyond_x, cells).astype(np.float32)
-    ax = np.concatenate([act_x[:, 0] + act_x[:, 1], act_x[:, 2] + act_x[:, 3]], axis=1).astype(np.float32)
+    ax = np.concatenate([act_x[:, 1], act_x[:, 3]], axis=1).astype(np.float32)
     ay = np.broadcast_to(act_y[..., None], act_y.shape + (128,)).astype(np.float32)
 
-    hg = ghost_fluxes(coarse_rows, ghost_rows, time_index, groups_x, place_x, cells)
 
     smem = pl.BlockSpec(memory_space=pltpu.SMEM)
-    xtile3 = pl.BlockSpec((tile, cells, cells_z), lambda i, p: (i, 0, 0))
-    xtile4 = pl.BlockSpec((3, tile, cells, cells_z), lambda i, p: (0, i, 0, 0))
-    xtile5 = pl.BlockSpec((5, tile, cells, cells_z), lambda i, p: (0, i, 0, 0))
-    xplane = pl.BlockSpec((5, 2, cells, cells_z), lambda i, p: (0, 0, 0, 0))
-    yplane = pl.BlockSpec((5, 2, tile, cells_z), lambda i, p: (0, 0, i, 0))
-    params = pltpu.CompilerParams(vmem_limit_bytes=vmem_bytes, dimension_semantics=("arbitrary",))
+    anywhere = pl.BlockSpec(memory_space=pl.ANY)
     planes = jax.ShapeDtypeStruct((5, 2, cells, cells_z), f32)
     whole = jax.ShapeDtypeStruct((5, cells, cells, cells_z), f32)
-
-    def fixed(table, which=None):
-        dims = table.shape[1:]
-        if which is None:
-            return pl.BlockSpec(table.shape, lambda i, p: (0,) * table.ndim)
-        return pl.BlockSpec((1,) + dims, lambda i, p: (p[which],) + (0,) * len(dims))
-
-    def call(kernel, in_specs, out_shape, out_specs, scratch, cost, grid=steps, **more):
-        return pl.pallas_call(
-            kernel,
-            grid_spec=pltpu.PrefetchScalarGridSpec(
-                num_scalar_prefetch=1, grid=(grid,), in_specs=in_specs, out_specs=out_specs,
-                scratch_shapes=scratch,
-            ),
-            out_shape=out_shape,
-            compiler_params=params,
-            cost_estimate=pl.CostEstimate(flops=cost[0], bytes_accessed=cost[1], transcendentals=0),
-            **more,
-        )
-
     size = 4 * 5 * cells * cells * cells_z
     rows = tile * cells
     bf16 = jnp.bfloat16
-    xlo, xhi, ylo, yhi = call(
-        functools.partial(edge_kernel, cells=cells, tile=tile, last=steps - 1),
-        [smem, smem, fixed(weights, 1), xtile3, xtile4, xtile3],
-        [planes] * 4,
-        [xplane, xplane, yplane, yplane],
-        [pltpu.VMEM((5, 2, tile, 8, 128), f32)],
-        (size * 20, size),
+    top = steps - 1
+
+    def spec(dims, axis=None, index=lambda i: i):
+        def place_of(i, *_):
+            return tuple(index(i) if d == axis else 0 for d in range(len(dims)))
+
+        return pl.BlockSpec(dims, place_of)
+
+    def fixed(table):
+        return spec(table.shape)
+
+    def state_specs(index):
+        return [
+            spec((tile, cells, cells_z), 0, index),
+            spec((3, tile, cells, cells_z), 1, index),
+            spec((tile, cells, cells_z), 0, index),
+        ]
+
+    def params(**more):
+        return pltpu.CompilerParams(
+            vmem_limit_bytes=vmem_bytes, dimension_semantics=("arbitrary",), **more
+        )
+
+    def cost(flops, moved):
+        return pl.CostEstimate(flops=flops, bytes_accessed=moved, transcendentals=0)
+
+    slots, width = ghost_rows.shape[2], coarse_rows.shape[3]
+    coarse = coarse_rows[:, :, 0, :].transpose(0, 2, 1)
+    same = lambda i: i
+    xlo, xhi, ylo, yhi, hg = pl.pallas_call(
+        functools.partial(edge_kernel, cells=cells, tile=tile, last=top, groups=groups_x),
+        grid=(steps,),
+        in_specs=[
+            smem, smem, fixed(weights), fixed(ghost_rows[0]), fixed(time_index[0]), fixed(coarse),
+            *state_specs(same),
+        ],
+        out_shape=[planes] * 4 + [jax.ShapeDtypeStruct((5, cells, slots), f32)],
+        out_specs=[
+            spec(planes.shape), spec(planes.shape),
+            spec((5, 2, tile, cells_z), 2), spec((5, 2, tile, cells_z), 2), spec((5, cells, slots)),
+        ],
+        scratch_shapes=[
+            pltpu.VMEM((5, 2, tile, 8, 128), f32),
+            pltpu.VMEM((slots, width), f32),
+            pltpu.VMEM((slots, width), f32),
+            pltpu.SemaphoreType.DMA((groups_x,)),
+            pltpu.SemaphoreType.DMA((groups_x,)),
+        ],
+        compiler_params=params(collective_id=0, has_side_effects=True),
+        cost_estimate=cost(size * 20, size),
         name="edges",
-    )(place, cx, cy, weights, density, momentum, energy)
-
-    def shift(array, axis, by):
-        peers = lax.axis_size(axis)
-        return lax.ppermute(
-            array, axis, [(i, i + by) for i in range(peers) if 0 <= i + by < peers]
-        )
-
-    in_xlo = shift(xhi, "gx", 1)
-    in_xhi = shift(xlo, "gx", -1)
-    in_ylo = shift(yhi, "gy", 1)
-    in_yhi = shift(ylo, "gy", -1)
-
-    top = steps - 1
-    acc = call(
+    )(cx, cy, weights, ghost_rows[0], time_index[0], coarse, density, momentum, energy)
+
+    acc, in_xlo, in_xhi, in_ylo, in_yhi = pl.pallas_call(
         functools.partial(lines_kernel, cells=cells, tile=tile, steps=steps),
-        [
-            fixed(mx, 0), fixed(my, 1), fixed(mz), fixed(wz), fixed(sx, 0), fixed(sy, 1), fixed(sz),
-            pl.BlockSpec((5, 8, rows), lambda i, p: (0, 0, jnp.minimum(i, top))),
-            pl.BlockSpec((tile, cells, cells_z), lambda i, p: (jnp.minimum(i, top), 0, 0)),
-            pl.BlockSpec((3, tile, cells, cells_z), lambda i, p: (0, jnp.minimum(i, top), 0, 0)),
-            pl.BlockSpec((tile, cells, cells_z), lambda i, p: (jnp.minimum(i, top), 0, 0)),
+        grid=(2 * steps,),
+        in_specs=[
+            fixed(mx), fixed(my), fixed(mz), fixed(wz), fixed(sx), fixed(sy), fixed(sz), fixed(hg),
+            *[anywhere] * 4, *state_specs(lambda i: jnp.minimum(i, top)),
         ],
-        whole,
-        pl.BlockSpec((5, cells, 8, cells_z), lambda i, p: (0, 0, jnp.maximum(i - steps, 0), 0)),
-        [
+        out_shape=[whole] + [planes] * 4,
+        out_specs=[
+            spec((5, cells, 8, cells_z), 2, lambda i: jnp.maximum(i - steps, 0)), *[anywhere] * 4
+        ],
+        scratch_shapes=[
+            pltpu.SemaphoreType.DMA((4,)),
+            pltpu.SemaphoreType.DMA((4,)),
+            pltpu.SemaphoreType.DMA((4,)),
             pltpu.VMEM((cells // 8, 5, 2 * cells * 8, cells_z), bf16),
             pltpu.VMEM((5, 2 * rows, cells_z), bf16),
             pltpu.VMEM((5, rows, 2 * cells_z), bf16),
@@ -448,17 +577,26 @@
             pltpu.VMEM((rows, 2 * rows), bf16),
             pltpu.VMEM((cells_z, cells_z), bf16),
         ],
-        (size * 1200, 2 * size),
-        grid=2 * steps,
+        compiler_params=params(collective_id=1, has_side_effects=True),
+        cost_estimate=cost(size * 1200, 2 * size),
         name="lines",
-    )(place, mx, my, mz, wz, sx, sy, sz, hg, density, momentum, energy)
-    return call(
-        functools.partial(join_kernel, cells=cells, tile=tile),
-        [smem, fixed(ay, 1), xtile5, xplane, xplane, yplane, yplane],
-        whole,
-        xtile5,
-        [],
-        (size * 4, 2 * size),
+    )(mx, my, mz, wz, sx, sy, sz, hg, xlo, xhi, ylo, yhi, density, momentum, energy)
+
+    return pl.pallas_call(
+        functools.partial(join_kernel, cells=cells, tile=tile, last=top, groups=groups_x),
+        grid_spec=pltpu.PrefetchScalarGridSpec(
+            num_scalar_prefetch=1,
+            grid=(steps,),
+            in_specs=[
+                smem, pl.BlockSpec((1, *ay.shape[1:]), lambda i, p: (p[1], 0, 0, 0)),
+                spec((5, tile, cells, cells_z), 1), spec(planes.shape), spec(planes.shape),
+                spec((5, 2, tile, cells_z), 2), spec((5, 2, tile, cells_z), 2),
+            ],
+            out_specs=spec((5, tile, cells, cells_z), 1),
+        ),
+        out_shape=whole,
+        compiler_params=params(),
+        cost_estimate=cost(size * 4, 2 * size),
         name="join",
     )(place, ax, ay, acc, in_xlo, in_xhi, in_ylo, in_yhi)
 

time: 126 us -> 75.6 us (0.60)
  blocking collectives: 50.8 us -> 0 us
  Pallas kernels: 50.3 us -> 74.8 us
  local copies, waits for them, and re-layouts: 10.6 us -> 0 us
  starting transfers between devices: 8.99 us -> 0 us
  matrix products: 2.98 us -> 0 us
    all_gather x1 -> x0, blocking collectives: 50.8 us -> none  [ghost_fluxes(): every = lax.all_gather(sent, 'gx')]
    pallas_call x3, Pallas kernels: 50.3 us -> 74.8 us  [the longest x1 46.7 us: local(): pl.pallas_call(functools.partial(lines_kernel, cells=cells, tile=tile, st...]
    ppermute x4 -> x0, starting transfers between devices: 8.99 us -> none  [shift(): lax.ppermute(array, axis, [(i, i + by) for i in range(peers) if 0 <= i +...]
    unnamed x31 -> x0, local copies, waits for them, and re-layouts: 7.01 us -> none
    dot_general x4 -> x0, matrix products: 2.98 us -> none  [the longest x1 1.23 us: ghost_fluxes(): old = jnp.dot(onehot, coarse_rows[0, :, 0, :], precision=highest)]
  transfers between devices with their start and end apart: 4 -> 0, of which waited for: 0 -> 0; matrix products, arithmetic and copies ran while one was open for 6% -> 0% of each run, Pallas kernels for 22% -> 0%
where the time goes in v4:
time: 75.6 us; the launch traced here: 75.4 us
  Pallas kernels  74.8 us (99%)
    pallas_call x1, Pallas kernels, local(): pl.pallas_call(functools.partial(lines_kernel, cells=cells, tile=tile, st...  46.7 us
    pallas_call x1, Pallas kernels, local(): pl.pallas_call(functools.partial(edge_kernel, cells=cells, tile=tile, las...  17.3 us
    pallas_call x1, Pallas kernels, local(): pl.pallas_call(functools.partial(join_kernel, cells=cells, tile=tile, las...  10.8 us

profile of v4, /device:TPU:0, one launch (start us, length us, event | category | flops | bytes accessed | tf_op | source)
XLA Modules:
  0.0 75.4 jit_solution(11486316810850127467)
XLA Ops:
  0.0 0.7 pad_add_fusion.place
  0.7 17.3 %edges.1 = (f32[5,2,32,512]{3,2,1,0:T(8,128)}, f32[5,2,32,512]{3,2,1,0:T(8,128)}, f32[5,2,32,512]{3,2,1,0:T(8,128)}, f32[5,2,32,512]{3,2,1,0:T(8,128)}, f32[5,32,128]{2,1,0:T(8,128)}) custom-call(f32[8,68]{1,0:T(8,128)} %constant.33.clone.cx, f32[4,68]{1,0:T(4,128)} %constant.34.clone.cy, f32[4,2,32,128]{3,2,1,0:T(8,128)} %constant.35.clone.weights, ...), custom_call_target="tpu_custom_call" | custom-call | flops 209715200 | bytes 10485760 | tf_op jit(solution)/shard_map/edges/pallas_call | solution.py:533
  17.9 46.7 %lines.1 = (f32[5,32,32,512]{3,2,1,0:T(8,128)}, f32[5,2,32,512]{3,2,1,0:T(8,128)}, f32[5,2,32,512]{3,2,1,0:T(8,128)}, f32[5,2,32,512]{3,2,1,0:T(8,128)}, f32[5,2,32,512]{3,2,1,0:T(8,128)}) custom-call(f32[8,256,256]{2,1,0:T(8,128)} %constant.36.clone.mx, f32[4,256,256]{2,1,0:T(8,128)} %constant.37.clone.my, f32[512,512]{1,0:T(8,128)} %constant.38.clone.mz, ...), custom_call_target="tpu_custom_call" | custom-call | flops 12582912000 | bytes 20971520 | tf_op jit(solution)/shard_map/lines/pallas_call | solution.py:557
  64.6 10.8 %join.1 = f32[5,32,32,512]{3,2,1,0:T(8,128)} custom-call(s32[2]{0:T(128)} %pad_add_fusion.place, f32[8,64]{1,0:T(8,128)} %constant.43.clone.ax, f32[4,4,32,128]{3,2,1,0:T(8,128)} %constant.44.clone.ay, f32[5,32,32,512]{3,2,1,0:T(8,128)} %get-tuple-element.20.acc, f32[5,2,32,512]{3,2,1,0:T(8,128)} %get-tuple-element.21.xlo, ...), custom_call_target="tpu_custom_call" | custom-call | flops 41943040 | bytes 20971520 | tf_op jit(solution)/shard_map/join/pallas_call | solution.py:585

commit v5 on v4

--- a/solution.py
+++ b/solution.py
@@ -292,7 +292,7 @@
 
 def lines_kernel(
     mx, my, mz, wz, sx, sy, sz, hg, to_low_x, to_high_x, to_low_y, to_high_y, rho, mom, ene,
-    out, low_x, high_x, low_y, high_y, send_sem, recv_sem, keep_sem,
+    out, low_x, high_x, low_y, high_y, send_sem, recv_sem,
     f_buf, g_buf, h_buf, acc, mx_buf, my_buf, mz_buf, *, cells, tile, steps
 ):
     step = pl.program_id(0)
@@ -315,27 +315,23 @@
             src_ref=source, dst_ref=target, send_sem=send_sem.at[n], recv_sem=recv_sem.at[n],
             device_id={axis: jnp.clip(here + by, 0, count - 1)}, device_id_type=pl.DeviceIdType.MESH,
         )
-        own = pltpu.make_async_copy(source, target, keep_sem.at[n])
-        moves.append((axis, here + by, sends, gets, copy, own))
+        moves.append((axis, here + by, sends, gets, copy))
 
     @pl.when(step == 0)
     def _():
         barrier = pltpu.get_barrier_semaphore()
-        for axis, to, sends, _, _, _ in moves:
+        for axis, to, sends, _, _ in moves:
             @pl.when(sends)
             def _():
                 pl.semaphore_signal(
                     barrier, inc=1, device_id={axis: to}, device_id_type=pl.DeviceIdType.MESH
                 )
-        pl.semaphore_wait(barrier, sum(jnp.where(gets, 1, 0) for _, _, _, gets, _, _ in moves))
-        for _, _, sends, gets, copy, own in moves:
+        pl.semaphore_wait(barrier, sum(jnp.where(gets, 1, 0) for _, _, _, gets, _ in moves))
+        for _, _, sends, gets, copy in moves:
             @pl.when(sends)
             def _():
                 copy.start()
 
-            @pl.when(jnp.logical_not(gets))
-            def _():
-                own.start()
         for buf, table in ((mx_buf, mx[lax.axis_index("gx")]), (my_buf, my[lax.axis_index("gy")])):
             buf[:, :rows] = table.astype(bf16)
             buf[:, rows:] = table.astype(bf16)
@@ -410,7 +406,7 @@
 
     @pl.when(step == 2 * steps - 1)
     def _():
-        for _, _, sends, gets, copy, own in moves:
+        for _, _, sends, gets, copy in moves:
             @pl.when(sends)
             def _():
                 copy.wait_send()
@@ -419,14 +415,10 @@
             def _():
                 copy.wait_recv()
 
-            @pl.when(jnp.logical_not(gets))
-            def _():
-                own.wait()
-
-
-def join_kernel(place, ax, ay, acc, xlo, xhi, ylo, yhi, out, *, cells, tile, last, groups):
+
+def join_kernel(place, ax, ay, acc, xlo, xhi, ylo, yhi, out, *, cells, tile, last, groups, groups_y):
     step = pl.program_id(0)
-    px = place[0]
+    px, py = place[0], place[1]
     zs = acc.shape[3] // 128
 
     def piece(n, _):
@@ -436,15 +428,18 @@
             ys = slice(yy, yy + 8)
             a_low, a_high = ay[0, 1, ys], ay[0, 3, ys]
             for f in range(5):
-                x_low, x_high = xlo[f, 1, ys, zc], xhi[f, 1, ys, zc]
+                x_low = jnp.where(px > 0, xlo[f, 1, ys, zc], 0.0)
+                x_high = jnp.where(px < groups - 1, xhi[f, 1, ys, zc], 0.0)
                 for x in range(tile):
                     row = slice(x, x + 1)
                     term = acc[f, x, ys, zc] + weights[x][0] * x_low + weights[x][1] * x_high
-                    term += a_low * ylo[f, 1, row, zc] + a_high * yhi[f, 1, row, zc]
+                    y_low = jnp.where(py > 0, ylo[f, 1, row, zc], 0.0)
+                    y_high = jnp.where(py < groups_y - 1, yhi[f, 1, row, zc], 0.0)
+                    term += a_low * y_low + a_high * y_high
                     if yy == 0:
-                        term += ay[0, 0, ys] * ylo[f, 0, row, zc]
+                        term += ay[0, 0, ys] * jnp.where(py > 0, ylo[f, 0, row, zc], 0.0)
                     if yy + 8 == cells:
-                        term += ay[0, 2, ys] * yhi[f, 0, row, zc]
+                        term += ay[0, 2, ys] * jnp.where(py < groups_y - 1, yhi[f, 0, row, zc], 0.0)
                     out[f, x, ys, zc] = term
         return 0
 
@@ -568,7 +563,6 @@
         scratch_shapes=[
             pltpu.SemaphoreType.DMA((4,)),
             pltpu.SemaphoreType.DMA((4,)),
-            pltpu.SemaphoreType.DMA((4,)),
             pltpu.VMEM((cells // 8, 5, 2 * cells * 8, cells_z), bf16),
             pltpu.VMEM((5, 2 * rows, cells_z), bf16),
             pltpu.VMEM((5, rows, 2 * cells_z), bf16),
@@ -583,7 +577,7 @@
     )(mx, my, mz, wz, sx, sy, sz, hg, xlo, xhi, ylo, yhi, density, momentum, energy)
 
     return pl.pallas_call(
-        functools.partial(join_kernel, cells=cells, tile=tile, last=top, groups=groups_x),
+        functools.partial(join_kernel, cells=cells, tile=tile, last=top, groups=groups_x, groups_y=groups_y),
         grid_spec=pltpu.PrefetchScalarGridSpec(
             num_scalar_prefetch=1,
             grid=(steps,),

time: 75.6 us -> 64.5 us (0.85)
  Pallas kernels: 74.8 us -> 63.7 us
    pallas_call x1, Pallas kernels: 46.7 us -> 35.1 us  [local(): pl.pallas_call(functools.partial(lines_kernel, cells=cells, tile=tile, st...]
where the time goes in v5:
time: 64.5 us; the launch traced here: 64.4 us
  Pallas kernels  63.7 us (99%)
  other arithmetic  0.66 us (1%)
    pallas_call x1, Pallas kernels, local(): pl.pallas_call(functools.partial(lines_kernel, cells=cells, tile=tile, st...  35.1 us
    pallas_call x1, Pallas kernels, local(): pl.pallas_call(functools.partial(edge_kernel, cells=cells, tile=tile, las...  17.3 us
    pallas_call x1, Pallas kernels, local(): pl.pallas_call(functools.partial(join_kernel, cells=cells, tile=tile, las...  11.3 us

profile of v5, /device:TPU:0, one launch (start us, length us, event | category | flops | bytes accessed | tf_op | source)
XLA Modules:
  0.0 64.4 jit_solution(12504297280740275050)
XLA Ops:
  0.0 0.7 %pad_add_fusion.place = s32[2]{0:T(128)} fusion(s32[1]{0:T(128)} %bitcast.1, s32[1]{0:T(128)} %bitcast), kind=kLoop, calls=%fused_computation | loop fusion | flops 2 | bytes 16 | tf_op jit(solution)/shard_map/stack | solution.py:463
  0.7 17.3 %edges.1 = (f32[5,2,32,512]{3,2,1,0:T(8,128)}, f32[5,2,32,512]{3,2,1,0:T(8,128)}, f32[5,2,32,512]{3,2,1,0:T(8,128)}, f32[5,2,32,512]{3,2,1,0:T(8,128)}, f32[5,32,128]{2,1,0:T(8,128)}) custom-call(f32[8,68]{1,0:T(8,128)} %constant.33.clone.cx, f32[4,68]{1,0:T(4,128)} %constant.34.clone.cy, f32[4,2,32,128]{3,2,1,0:T(8,128)} %constant.35.clone.weights, ...), custom_call_target="tpu_custom_call" | custom-call | flops 209715200 | bytes 10485760 | tf_op jit(solution)/shard_map/edges/pallas_call | solution.py:528
  17.9 35.1 %lines.1 = (f32[5,32,32,512]{3,2,1,0:T(8,128)}, f32[5,2,32,512]{3,2,1,0:T(8,128)}, f32[5,2,32,512]{3,2,1,0:T(8,128)}, f32[5,2,32,512]{3,2,1,0:T(8,128)}, f32[5,2,32,512]{3,2,1,0:T(8,128)}) custom-call(f32[8,256,256]{2,1,0:T(8,128)} %constant.36.clone.mx, f32[4,256,256]{2,1,0:T(8,128)} %constant.37.clone.my, f32[512,512]{1,0:T(8,128)} %constant.38.clone.mz, ...), custom_call_target="tpu_custom_call" | custom-call | flops 12582912000 | bytes 20971520 | tf_op jit(solution)/shard_map/lines/pallas_call | solution.py:552
  53.0 11.3 %join.1 = f32[5,32,32,512]{3,2,1,0:T(8,128)} custom-call(s32[2]{0:T(128)} %pad_add_fusion.place, f32[8,64]{1,0:T(8,128)} %constant.43.clone.ax, f32[4,4,32,128]{3,2,1,0:T(8,128)} %constant.44.clone.ay, f32[5,32,32,512]{3,2,1,0:T(8,128)} %get-tuple-element.20.acc, f32[5,2,32,512]{3,2,1,0:T(8,128)} %get-tuple-element.21.xlo, ...), custom_call_target="tpu_custom_call" | custom-call | flops 41943040 | bytes 20971520 | tf_op jit(solution)/shard_map/join/pallas_call | solution.py:579
